TPU v7x, 32 devices: a whole 2x2x4 slice. The times are simulated.
32 devices in a mesh: src: 4 (over x, core), rcv: 8 (over z, y).
Axes of the slice: x: 2, y: 2, z: 4, core: 2. Of those that a mesh axis runs over, the one named last changes fastest.
Arguments:
- traces: bfloat16 [1024, 16, 2000], P('rcv', 'src')
- src_index: int32 [256], P('src'), may hold values from 0 to 1023, as said below
- quality: int32 [1024, 16], P('rcv'), may hold values 0 or 1
Outputs:
- xcorr: float32 [256, 201, 1024], P('src', None, 'rcv')
Inputs may be any that keep to these rules, and one draw needn't show every extreme that they name: `src_index`: the source numbered j within each group of 64 sources lies in receiver block j mod 8, among channels (j mod 8) * 128 up to that plus 128 - 1.
All inputs are finite; a program needn't handle non-finite values. No bound on the sum of `quality` on one device may be relied on, other than what follows from the above.
Results may differ from a plain program's by a relative error of at most 0.0067.
Values may be sent and summed in bfloat16 or wider, within the bound.
A program may use at most 576 MiB of HBM per device.

v0:
```python
import math

import jax
import jax.numpy as jnp
from jax import lax
from jax.sharding import PartitionSpec as P

LAGH = 100


def make_tables(length):
    half = length // 2
    bins = jnp.arange(1, half + 1, dtype=jnp.int32)
    times = jnp.arange(length, dtype=jnp.int32)
    phase = (times[:, None] * bins[None, :] % length).astype(jnp.float32) * (2.0 * math.pi / length)
    forward = jnp.concatenate([jnp.cos(phase), -jnp.sin(phase)], axis=1).astype(jnp.bfloat16)
    lagvals = jnp.arange(-LAGH, LAGH + 1, dtype=jnp.int32)
    phase_lag = (bins[:, None] * lagvals[None, :] % length).astype(jnp.float32) * (
        2.0 * math.pi / length
    )
    weights = jnp.where(bins == half, 1.0, 2.0).astype(jnp.float32)[:, None] / jnp.sqrt(
        jnp.float32(half)
    )
    inverse = jnp.concatenate(
        [weights * jnp.cos(phase_lag), -weights * jnp.sin(phase_lag)], axis=0
    ).astype(jnp.bfloat16)
    return (forward, inverse)


def whiten(samples, forward):
    length = samples.shape[2]
    half = length // 2
    spec = jnp.dot(samples.reshape(-1, length), forward, preferred_element_type=jnp.float32)
    real_part = spec[:, :half]
    imag_part = spec[:, half:]
    power = real_part * real_part + imag_part * imag_part
    level = 0.5 * jnp.sqrt(jnp.mean(power, axis=1, keepdims=True) + 1e-06)
    denom = jnp.maximum(jnp.sqrt(power), level)
    white = jnp.concatenate([real_part / denom, imag_part / denom], axis=1).astype(jnp.bfloat16)
    return white.reshape(samples.shape[0], samples.shape[1], length)


def on_device(traces, src_index, quality):
    rows, seg_local, length = traces.shape
    half = length // 2
    nsrc = src_index.shape[0]
    seg_all = quality.shape[1]
    forward, inverse = make_tables(length)
    white_local = whiten(traces, forward)
    white_all = lax.all_gather(white_local, "src", axis=1, tiled=True)
    qual = quality.astype(jnp.bfloat16)
    first_channel = lax.axis_index("rcv") * rows
    onehot = (
        src_index[:, None] == first_channel + jnp.arange(rows, dtype=jnp.int32)[None, :]
    ).astype(jnp.bfloat16)
    found = jnp.dot(onehot, white_all.reshape(rows, -1), preferred_element_type=jnp.float32)
    flags = jnp.dot(onehot, qual, preferred_element_type=jnp.float32)
    found, flags = (
        lax.psum(found.astype(jnp.bfloat16), "rcv").astype(jnp.float32),
        lax.psum(flags.astype(jnp.bfloat16), "rcv").astype(jnp.float32),
    )
    srcw = found.reshape(nsrc, seg_all, length).astype(jnp.bfloat16)
    msrc = flags.astype(jnp.bfloat16)
    count = jnp.dot(msrc, qual.T, preferred_element_type=jnp.float32)
    recv = white_all * qual[:, :, None]
    recv_re = recv[:, :, :half]
    recv_im = recv[:, :, half:]
    left_all = srcw * msrc[:, :, None]
    group = 8
    left_blocks = left_all.reshape(nsrc // group, group, seg_all, length)

    def one_block(left):
        left_re = left[:, :, :half]
        left_im = left[:, :, half:]
        pre = jnp.einsum("isk,jsk->ijk", left_re, recv_re, preferred_element_type=jnp.float32)
        pre = pre + jnp.einsum("isk,jsk->ijk", left_im, recv_im, preferred_element_type=jnp.float32)
        pim = jnp.einsum("isk,jsk->ijk", left_im, recv_re, preferred_element_type=jnp.float32)
        pim = pim - jnp.einsum("isk,jsk->ijk", left_re, recv_im, preferred_element_type=jnp.float32)
        cross = jnp.concatenate([pre, pim], axis=2).astype(jnp.bfloat16)
        return jnp.einsum("ijk,kt->itj", cross, inverse, preferred_element_type=jnp.float32)

    lagged = lax.map(one_block, left_blocks)
    lagged = lagged.reshape(nsrc, 2 * LAGH + 1, rows)
    return lagged / jnp.maximum(count, 1.0)[:, None, :]


def solution(mesh):
    return jax.shard_map(
        on_device,
        mesh=mesh,
        in_specs=(P("rcv", "src", None), P("src"), P("rcv", None)),
        out_specs=P("src", None, "rcv"),
        check_vma=False,
    )
```

profile of v0, /device:TPU:0, one launch (start us, length us, event | category | flops | bytes accessed | tf_op | source)
XLA Modules:
  0.0 1466.2 jit_solution(3606919043101732945)
XLA Ops:
  6.5 35.3 %cosine_convert_fusion = (bf16[2000,1000]{1,0:T(8,128)(2,1)}, bf16[2000,1000]{1,0:T(8,128)(2,1)}) fusion(s32[1000]{0:T(1024)S(1)} %iota_add_fusion), kind=kLoop, calls=%fused_computation.36 | loop fusion | flops 24000000 | bytes 8004000 | tf_op jit(solution)/shard_map/convert.10
  41.9 3.4 copy.17
  47.6 10.1 fusion.37
  62.1 2.8 pad_maximum_fusion.1
  64.9 3.0 copy.20
  67.9 60.0 %all-gather.2.cloned.1.call-done = bf16[128,16,2000]{0,2,1:T(8,128)(2,1)} async-done(((bf16[128,4,2000]{0,2,1:T(8,128)(2,1)}), bf16[128,16,2000]{0,2,1:T(8,128)(2,1)}) %all-gather.2.cloned.1.call-update) | async-done | bytes 8192016 | tf_op jit(solution)/shard_map/all_gather | solution.py:50
  127.9 8.3 convolution_convert_fusion
  136.2 9.6 convert_element_type.35
  145.8 31.0 %copy.21 = bf16[8,8,16,2000]{2,1,3,0:T(8,128)(2,1)} copy(bf16[8,8,16,2000]{3,2,1,0:T(8,128)(2,1)} %convert_element_type.35) | data formatting | bytes 8192000 | tf_op jit(solution)/shard_map/convert_element_type | solution.py:62
  177.7 22.0 %psum.15 = bf16[64,16]{0,1:T(8,128)(2,1)S(1)} all-reduce(bf16[64,16]{0,1:T(8,128)(2,1)S(1)} %convolution_convert_fusion.1), channel_id=1, replica_groups=mesh['src'=4,'rcv'=8] {'rcv'}, use_global_device_ids=true, to_apply=%region_2.3 | all-reduce | flops 1024 | bytes 4096 | tf_op jit(solution)/shard_map/psum | solution.py:60
  200.6 3.7 multiply_convert_fusion.1
  205.5 7.3 broadcast_multiply_fusion.1
  212.8 3.7 fusion.54
  216.5 2.5 copy.23
  219.0 2.5 copy.24
  221.5 911.6 %all-reduce.2.cloned.1.call-done = bf16[8,8,16,2000]{2,1,3,0:T(8,128)(2,1)} async-done(((bf16[8,8,16,2000]{2,1,3,0:T(8,128)(2,1)}), bf16[8,8,16,2000]{2,1,3,0:T(8,128)(2,1)}) %all-reduce.2.cloned.1.call-update) | async-done | bytes 4096016 | tf_op jit(solution)/shard_map/psum | solution.py:59
  1133.2 22.5 %broadcast_multiply_fusion = bf16[8,8,16,2000]{2,1,3,0:T(8,128)(2,1)} fusion(bf16[8,8,16,2000]{2,1,3,0:T(8,128)(2,1)} %all-reduce.2.cloned.1.call-done, bf16[8,8,16]{2,1,0:T(8,128)(2,1)S(1)} %bitcast.91), kind=kLoop, calls=%fused_computation.27 | loop fusion | flops 2048000 | bytes 8194048 | tf_op jit(solution)/shard_map/mul | solution.py:68
  1155.7 296.3 %while.10 = (s32[]{:T(128)}, f32[8,8,201,128]{3,1,0,2:T(8,128)}, bf16[8,8,16,2000]{2,1,3,0:T(8,128)(2,1)}, bf16[128,16,1000]{0,1,2:T(8,128)(2,1)}, bf16[128,16,1...) while((s32[]{:T(128)}, f32[8,8,201,128]{3,1,0,2:T(8,128)}, ...), condition=%wide.region_4.5_spmd, body=%wide.region_3.4_spmd.sunk | while | flops 960512000 | bytes 119130632 | solution.py:82
  1166.5 2.5 fusion.110
  1171.1 2.5 fusion.112
  1174.4 2.5 fusion.113
  1177.0 2.3 fusion.114
  1180.7 2.5 fusion.116
  1185.6 14.2 pad_maximum_fusion.4
  1202.1 2.5 fusion.110
  1206.7 2.5 fusion.112
  1210.1 2.5 fusion.113
  1212.7 2.3 fusion.114
  1216.3 2.5 fusion.116
  1221.3 14.2 pad_maximum_fusion.4
  1237.8 2.5 fusion.110
  1242.4 2.5 fusion.112
  1245.8 2.5 fusion.113
  1248.3 2.3 fusion.114
  1252.0 2.5 fusion.116
  1257.0 14.2 pad_maximum_fusion.4
  1273.5 2.5 fusion.110
  1278.1 2.5 fusion.112
  1281.5 2.5 fusion.113
  1284.1 2.3 fusion.114
  1287.7 2.5 fusion.116
  1292.7 14.2 pad_maximum_fusion.4
  1309.2 2.5 fusion.110
  1313.8 2.5 fusion.112
  1317.2 2.5 fusion.113
  1319.8 2.3 fusion.114
  1323.4 2.5 fusion.116
  1328.4 14.2 pad_maximum_fusion.4
  1344.9 2.5 fusion.110
  1349.5 2.5 fusion.112
  1352.9 2.5 fusion.113
  1359.1 2.5 fusion.116
  1364.1 14.2 pad_maximum_fusion.4
  1380.6 2.5 fusion.110
  1385.2 2.5 fusion.112
  1388.6 2.5 fusion.113
  1394.8 2.5 fusion.116
  1399.8 14.2 pad_maximum_fusion.4
  1416.3 2.5 fusion.110
  1420.9 2.5 fusion.112
  1424.3 2.5 fusion.113
  1430.5 2.5 fusion.116
  1435.5 14.2 pad_maximum_fusion.4
  1452.0 7.2 bitcast_divide_fusion
  (151 shorter events, 88.3 us)
Async XLA Ops:
  6.5 121.4 %all-gather.2.cloned.1.call-start = ((), (), s32[]{:S(2)}) async-start(), calls=%async_computation | async-start | bytes 10240000 | tf_op jit(solution)/shard_map/all_gather | solution.py:50
  64.8 63.1 %copy-start.7 = (s32[64]{0:T(128)S(1)}, s32[64]{0:T(128)}, u32[]{:S(2)}) copy-start(s32[64]{0:T(128)} %param.6) | copy-start | bytes 772
  67.9 1065.3 %all-reduce.2.cloned.1.call-start = ((), (), s32[]{:S(2)}) async-start(), calls=%async_computation.1 | async-start | bytes 65536000 | tf_op jit(solution)/shard_map/psum | solution.py:59
  176.8 0.7 copy-start.6
  1155.7 296.3 %copy-start.5 = (f32[64,128]{1,0:T(8,128)S(1)}, f32[64,128]{1,0:T(8,128)}, u32[]{:S(2)}) copy-start(f32[64,128]{1,0:T(8,128)} %convolution_maximum_fusion) | copy-start | bytes 98308
  1166.5 3.4 copy-start.1
  1171.1 3.4 copy-start.3
  1180.7 3.4 copy-start.2
  1184.0 1.6 copy-start
  1185.6 14.3 copy-start.4
  1202.1 3.4 copy-start.1
  1206.7 3.4 copy-start.3
  1216.3 3.4 copy-start.2
  1219.7 1.6 copy-start
  1221.3 14.3 copy-start.4
  1237.8 3.4 copy-start.1
  1242.4 3.4 copy-start.3
  1252.0 3.4 copy-start.2
  1255.4 1.6 copy-start
  1257.0 14.3 copy-start.4
  1273.5 3.4 copy-start.1
  1278.1 3.4 copy-start.3
  1287.7 3.4 copy-start.2
  1291.1 1.6 copy-start
  1292.7 14.3 copy-start.4
  1309.2 3.4 copy-start.1
  1313.8 3.4 copy-start.3
  1323.4 3.4 copy-start.2
  1326.8 1.6 copy-start
  1328.4 14.3 copy-start.4
  1344.9 3.4 copy-start.1
  1349.5 3.4 copy-start.3
  1359.1 3.4 copy-start.2
  1362.5 1.6 copy-start
  1364.1 14.3 copy-start.4
  1380.6 3.4 copy-start.1
  1385.2 3.4 copy-start.3
  1394.8 3.4 copy-start.2
  1398.2 1.6 copy-start
  1399.8 14.3 copy-start.4
  1416.3 3.4 copy-start.1
  1420.9 3.4 copy-start.3
  1430.5 3.4 copy-start.2
  1433.9 1.6 copy-start
  1435.5 14.3 copy-start.4
Sparse Core Ops, SparseCore 0:
  68.0 59.8 all-gather.1
  177.0 956.1 all-reduce.1
where the time goes:
time: 1470 us
  waiting for transfers between devices  972 us (66%)
  other arithmetic  195 us (13%)
  local copies, waits for them, and re-layouts  174 us (12%)
  matrix products  77.6 us (5%)
  blocking collectives  22 us (1%)
    psum x1, waiting for transfers between devices, on_device(): lax.psum(found.astype(jnp.bfloat16), 'rcv').astype(jnp.float32)  912 us
    concatenate x8, other arithmetic, one_block(): cross = jnp.concatenate([pre, pim], axis=2).astype(jnp.bfloat16)  114 us
    all_gather x1, waiting for transfers between devices, on_device(): white_all = lax.all_gather(white_local, 'src', axis=1, tiled=True)  60 us
    convert_element_type x2, local copies, waits for them, and re-layouts, on_device(): srcw = found.reshape(nsrc, seg_all, length).astype(jnp.bfloat16)  40.6 us
    another operation x3, other arithmetic  40 us
  transfers between devices with their start and end apart: 2, of which 2 were waited for; matrix products, arithmetic and copies ran while one was open for 1% of the time, Pallas kernels for 0%

commit v1 on v0

v1 whole, which is shorter than its diff:
```python
import functools
import math

import jax
import jax.numpy as jnp
import ml_dtypes
import numpy as np
from jax import lax
from jax.experimental import pallas as pl
from jax.experimental.pallas import tpu as pltpu
from jax.sharding import PartitionSpec as P

LAGH = 100
BINS = 8
GROUPS_STEP = 16
VMEM = 60 * 1024 * 1024


def padded_groups(length):
    groups = -(-(length // 2) // BINS)
    return -(-groups // GROUPS_STEP) * GROUPS_STEP


def make_tables(length):
    half = length // 2
    pad = padded_groups(length) * BINS
    bins = np.arange(1, half + 1)
    unit = np.float32(2.0 * math.pi / length)
    phase = (bins[:, None] * np.arange(length)[None, :] % length).astype(np.float32) * unit
    forward = np.zeros((2, pad, length), np.float32)
    forward[0, :half] = np.cos(phase)
    forward[1, :half] = -np.sin(phase)
    lags = np.arange(-LAGH, LAGH + 1)
    phase = (lags[:, None] * bins[None, :] % length).astype(np.float32) * unit
    weights = np.where(bins == half, 1.0, 2.0).astype(np.float32) / np.sqrt(np.float32(half))
    nlag = 2 * LAGH + 1
    inverse = np.zeros((-(-nlag // 16) * 16, 2, pad), np.float32)
    inverse[:nlag, 0, :half] = weights * np.cos(phase)
    inverse[:nlag, 1, :half] = -weights * np.sin(phase)
    step = GROUPS_STEP * BINS
    inverse = inverse.reshape(-1, 2, pad // step, step).transpose(0, 2, 1, 3)
    inverse = inverse.reshape(-1, 2 * pad)
    return forward.astype(ml_dtypes.bfloat16), inverse.astype(ml_dtypes.bfloat16)


def whiten_kernel(half, seg, forward_ref, traces_ref, quality_ref, out_ref, spec, power):
    step = pl.program_id(0)
    rows = forward_ref.shape[1]
    cols = traces_ref.shape[0]
    width = cols // seg
    part = lax.dot_general(
        forward_ref[...].reshape(2 * rows, -1),
        traces_ref[...],
        (((1,), (1,)), ((), ())),
        preferred_element_type=jnp.float32,
    )
    re, im = part[:rows], part[rows:]
    start = pl.multiple_of(step * rows, rows)
    spec[0, pl.ds(start, rows), :] = re
    spec[1, pl.ds(start, rows), :] = im
    total = jnp.sum((re * re + im * im).reshape(rows // 8, 8, cols), axis=0)

    @pl.when(step == 0)
    def _():
        power[...] = total

    @pl.when(step > 0)
    def _():
        power[...] += total

    @pl.when(step == pl.num_programs(0) - 1)
    def _():
        mean = jnp.sum(power[...], axis=0, keepdims=True) * (1.0 / half)
        level = 0.5 * jnp.sqrt(mean + 1e-06)
        qual = quality_ref[...]

        def one_group(g, carry):
            at = pl.ds(pl.multiple_of(g * BINS, BINS), BINS)
            re, im = spec[0, at, :], spec[1, at, :]
            scale = qual / jnp.maximum(jnp.sqrt(re * re + im * im), level)
            parts = []
            for value in (re * scale, im * scale):
                for s in range(seg):
                    parts.append(value[:, s * width : (s + 1) * width])
            out_ref[g] = jnp.concatenate(parts, axis=0).astype(jnp.bfloat16)
            return carry

        lax.fori_loop(0, out_ref.shape[0], one_group, 0, unroll=4)


def whiten(traces, quality_local, forward):
    rows, seg, length = traces.shape
    pad = forward.shape[1]
    steps = 4
    cols = rows * seg
    return pl.pallas_call(
        functools.partial(whiten_kernel, length // 2, seg),
        grid=(steps,),
        in_specs=[
            pl.BlockSpec((2, pad // steps, length), lambda i: (0, i, 0)),
            pl.BlockSpec((cols, length), lambda i: (0, 0)),
            pl.BlockSpec((1, cols), lambda i: (0, 0)),
        ],
        out_specs=pl.BlockSpec((pad // BINS, 2 * seg * BINS, rows), lambda i: (0, 0, 0)),
        out_shape=jax.ShapeDtypeStruct((pad // BINS, 2 * seg * BINS, rows), jnp.bfloat16),
        scratch_shapes=[
            pltpu.VMEM((2, pad, cols), jnp.float32),
            pltpu.VMEM((8, cols), jnp.float32),
        ],
        compiler_params=pltpu.CompilerParams(vmem_limit_bytes=VMEM),
        name="whiten",
    )(forward, traces.transpose(1, 0, 2).reshape(cols, length), quality_local)


def pick_kernel(onehot_ref, white_ref, out_ref):
    depth = white_ref.shape[0] * white_ref.shape[2]
    for g in range(white_ref.shape[1]):
        block = white_ref[:, g].reshape(depth, -1)
        out_ref[:, g * depth : (g + 1) * depth] = lax.dot_general(
            onehot_ref[...], block, (((1,), (1,)), ((), ())), preferred_element_type=jnp.float32
        )


def pick(onehot, white):
    parts, groups, depth, rows = white.shape
    step = GROUPS_STEP
    return pl.pallas_call(
        pick_kernel,
        grid=(groups // step,),
        in_specs=[
            pl.BlockSpec(onehot.shape, lambda i: (0, 0)),
            pl.BlockSpec((parts, step, depth, rows), lambda i: (0, i, 0, 0)),
        ],
        out_specs=pl.BlockSpec((onehot.shape[0], step * parts * depth), lambda i: (0, i)),
        out_shape=jax.ShapeDtypeStruct((onehot.shape[0], groups * parts * depth), jnp.float32),
        compiler_params=pltpu.CompilerParams(vmem_limit_bytes=VMEM),
        name="pick",
    )(onehot, white)


def correlate_kernel(blocks, white_ref, src_ref, flags_ref, qual_ref, inverse_ref, out_ref, cross):
    step = pl.program_id(0)
    parts, groups, depth, width = white_ref.shape
    full = parts * depth
    nsrc = src_ref.shape[0]
    each = nsrc // blocks
    nlag = out_ref.shape[1]
    half_k = groups * BINS
    lane = lax.broadcasted_iota(jnp.int32, (1, BINS, full), 2)
    row = lax.broadcasted_iota(jnp.int32, (1, BINS, full), 1)
    mask = lane % BINS == row

    def two_groups(t, carry):
        products = []
        for gg in range(2):
            g = 2 * t + gg
            y = white_ref[:, g].reshape(parts, 2, depth // 2, width)
            turned = jnp.concatenate([-y[:, 1:], y[:, :1]], axis=1)
            right = jnp.concatenate([y.reshape(full, width), turned.reshape(full, width)], axis=1)
            x = src_ref[:, pl.ds(pl.multiple_of(g * full, full), full)].astype(jnp.float32)
            left = jnp.where(mask, x[:, None, :], 0.0)
            left = left.reshape(nsrc * BINS, full).astype(jnp.bfloat16)
            prod = jnp.dot(left, right, preferred_element_type=jnp.float32)
            products.append(prod.reshape(nsrc, BINS, 2 * width))
        both = jnp.concatenate(products, axis=1).astype(jnp.bfloat16)
        at = pl.multiple_of(t * 2 * BINS, 2 * BINS)
        cross[:, pl.ds(at, 2 * BINS), :] = both[:, :, :width]
        cross[:, pl.ds(half_k + at, 2 * BINS), :] = both[:, :, width:]
        return carry

    lax.fori_loop(0, groups // 2, two_groups, 0)

    table = inverse_ref[...]

    def place(m):
        return (m % each) * blocks + m // each

    def add_pair(p, first):
        right = jnp.concatenate([cross[2 * p], cross[2 * p + 1]], axis=1)
        lagged = jnp.dot(table, right, preferred_element_type=jnp.float32)
        for h in range(2):
            value = lagged[:nlag, h * width : (h + 1) * width]
            i = place(2 * p + h)
            out_ref[i] = value if first else out_ref[i] + value

    @pl.when(step == 0)
    def _():
        lax.fori_loop(0, nsrc // 2, lambda p, c: (add_pair(p, True), c)[1], 0)

    @pl.when(step > 0)
    def _():
        lax.fori_loop(0, nsrc // 2, lambda p, c: (add_pair(p, False), c)[1], 0)

    @pl.when(step == pl.num_programs(0) - 1)
    def _():
        count = jnp.dot(flags_ref[...], qual_ref[...], preferred_element_type=jnp.float32)
        inv = 1.0 / jnp.maximum(count, 1.0)
        for m in range(nsrc):
            i = place(m)
            out_ref[i] = out_ref[i] * inv[m : m + 1, :]


def correlate(white, src, qual, inverse, blocks):
    parts, groups, depth, rows = white.shape
    nsrc = src.shape[0]
    step = GROUPS_STEP
    nlag = 2 * LAGH + 1
    taps = inverse.shape[0]
    flops = 2 * nsrc * rows * groups * (BINS * parts * depth * 2 + 2 * BINS * taps)
    return pl.pallas_call(
        functools.partial(correlate_kernel, blocks),
        grid=(groups // step,),
        in_specs=[
            pl.BlockSpec((parts, step, depth, rows), lambda i: (0, i, 0, 0)),
            pl.BlockSpec((nsrc, step * parts * depth), lambda i: (0, i)),
            pl.BlockSpec((nsrc, qual.shape[0]), lambda i: (0, groups * parts * depth // 128)),
            pl.BlockSpec(qual.shape, lambda i: (0, 0)),
            pl.BlockSpec((taps, 2 * step * BINS), lambda i: (0, i)),
        ],
        out_specs=pl.BlockSpec((nsrc, nlag, rows), lambda i: (0, 0, 0)),
        out_shape=jax.ShapeDtypeStruct((nsrc, nlag, rows), jnp.float32),
        scratch_shapes=[pltpu.VMEM((nsrc, 2 * step * BINS, rows), jnp.bfloat16)],
        compiler_params=pltpu.CompilerParams(vmem_limit_bytes=VMEM),
        cost_estimate=pl.CostEstimate(flops=flops, bytes_accessed=40_000_000, transcendentals=0),
        name="correlate",
    )(white, src, src, qual, inverse)


def on_device(blocks, traces, src_index, quality):
    rows, seg_local, length = traces.shape
    nsrc = src_index.shape[0]
    each = nsrc // blocks
    forward, inverse = make_tables(length)
    here, part = lax.axis_index("rcv"), lax.axis_index("src")
    mine = lax.dynamic_slice_in_dim(quality, part * seg_local, seg_local, axis=1)
    mine = mine.astype(jnp.float32).T.reshape(1, rows * seg_local)
    white_local = whiten(traces, mine, jnp.asarray(forward))
    white_all = lax.all_gather(white_local, "src", axis=0)
    own = lax.dynamic_index_in_dim(src_index.reshape(each, blocks), here, 1, keepdims=False)
    onehot = (own[:, None] == here * rows + jnp.arange(rows, dtype=jnp.int32)[None, :]).astype(
        jnp.bfloat16
    )
    qual = jnp.pad(quality.astype(jnp.bfloat16), ((0, 0), (0, 128 - quality.shape[1])))
    found = pick(onehot, white_all)
    flags = jnp.dot(onehot, qual, preferred_element_type=jnp.float32)
    sent = jnp.concatenate([found, flags], axis=1).astype(jnp.bfloat16)
    got = lax.all_gather(sent, "rcv", axis=0, tiled=True)
    return correlate(white_all, got, qual.T, jnp.asarray(inverse), blocks)


def solution(mesh):
    return jax.shard_map(
        functools.partial(on_device, mesh.shape["rcv"]),
        mesh=mesh,
        in_specs=(P("rcv", "src", None), P("src"), P("rcv", None)),
        out_specs=P("src", None, "rcv"),
        check_vma=False,
    )
```

time: 1470 us -> 259 us (0.18)
  waiting for transfers between devices: 972 us -> 133 us
  other arithmetic: 195 us -> 3.32 us
  local copies, waits for them, and re-layouts: 174 us -> 13.2 us
  Pallas kernels: 0 us -> 96 us
  matrix products: 77.6 us -> 0.19 us
  blocking collectives: 22 us -> 0 us
    psum x1 -> x0, waiting for transfers between devices: 912 us -> none  [on_device(): lax.psum(found.astype(jnp.bfloat16), 'rcv').astype(jnp.float32)]
    concatenate x10 -> x1, other arithmetic: 118 us -> 0.83 us  [on_device(): sent = jnp.concatenate([found, flags], axis=1).astype(jnp.bfloat16)]
    pallas_call x0 -> x3, Pallas kernels: none -> 96 us  [the longest x1 77.2 us: correlate(): pl.pallas_call(functools.partial(correlate_kernel, blocks), grid=(groups...]
    dot_general x32 -> x0, local copies, waits for them, and re-layouts: 78.7 us -> none  [the longest x8 20 us: one_block(): jnp.einsum('isk,jsk->ijk', left_re, recv_re, preferred_element_type=jnp.f...]
    dot_general x43 -> x0, matrix products: 77.4 us -> none  [the longest x8 20.3 us: one_block(): jnp.einsum('isk,jsk->ijk', left_re, recv_im, preferred_element_type=jnp.f...]
    all_gather x1 -> x2, waiting for transfers between devices: 60 us -> 133 us  [the longest x1 73.1 us: on_device(): got = lax.all_gather(sent, 'rcv', axis=0, tiled=True)]
    convert_element_type x2 -> x0, local copies, waits for them, and re-layouts: 40.6 us -> none  [on_device(): srcw = found.reshape(nsrc, seg_all, length).astype(jnp.bfloat16)]
    another operation x3 -> x1, other arithmetic: 40 us -> 1.28 us
where the time goes in v1:
time: 259 us
  waiting for transfers between devices  133 us (51%)
  Pallas kernels  96 us (37%)
  between operations  13.4 us (5%)
  local copies, waits for them, and re-layouts  13.2 us (5%)
  other arithmetic  3.32 us (1%)
    pallas_call x1, Pallas kernels, correlate(): pl.pallas_call(functools.partial(correlate_kernel, blocks), grid=(groups...  77.2 us
    all_gather x1, waiting for transfers between devices, on_device(): got = lax.all_gather(sent, 'rcv', axis=0, tiled=True)  73.1 us
    all_gather x1, waiting for transfers between devices, on_device(): white_all = lax.all_gather(white_local, 'src', axis=0)  59.5 us
    pallas_call x1, Pallas kernels, whiten(): pl.pallas_call(functools.partial(whiten_kernel, length // 2, seg), grid=(...  10.8 us
    pallas_call x1, Pallas kernels, pick(): pl.pallas_call(pick_kernel, grid=(groups // step,), in_specs=[pl.BlockSpe...  8.09 us
    pallas_call x1, local copies, waits for them, and re-layouts, correlate(): pl.pallas_call(functools.partial(correlate_kernel, blocks), grid=(groups...  7.85 us
  transfers between devices with their start and end apart: 2, of which 2 were waited for; matrix products, arithmetic and copies ran while one was open for 1% of the time, Pallas kernels for 0%

profile of v1, /device:TPU:0, one launch (start us, length us, event | category | flops | bytes accessed | tf_op | source)
XLA Modules:
  0.0 258.8 jit_solution(10989174552885649920)
XLA Ops:
  6.5 0.0 copy-start
  6.5 0.0 all-gather.6.cloned.1.call-start
  6.5 3.9 %copy.10 = bf16[4,128,2000]{2,1,0:T(8,128)(2,1)} copy(bf16[4,128,2000]{1,2,0:T(8,128)(2,1)} %bitcast.11) | data formatting | bytes 4096000 | tf_op jit(solution)/shard_map/transpose | solution.py:112
  10.4 0.0 copy-done
  10.4 0.6 dynamic-slice_convert_fusion
  11.0 10.8 %whiten.1 = bf16[128,64,128]{2,1,0:T(8,128)(2,1)} custom-call(bf16[2,1024,2000]{2,1,0:T(8,128)(2,1)} %constant.27.clone.forward_ref, bf16[512,2000]{1,0:T(8,128)(2,1)} %bitcast.10, f32[1,512]{1,0:T(1,128)} %bitcast.12), custom_call_target="tpu_custom_call" | custom-call | tf_op jit(solution)/shard_map/whiten/pallas_call | solution.py:96
  21.8 0.0 copy-start.1
  21.8 0.0 all-gather.6.cloned.1.call-update
  21.8 0.0 all-gather.4.cloned.1.call-start
  21.9 0.6 copy-done.1
  22.5 0.1 reshape.16
  22.5 0.2 dynamic-slice_reduce_fusion
  22.7 0.6 compare_convert_fusion.onehot_ref
  23.3 0.2 convolution_convert_fusion
  23.5 59.5 %all-gather.6.cloned.1.call-done = bf16[512,64,128]{2,1,0:T(8,128)(2,1)} async-done(((bf16[128,64,128]{2,1,0:T(8,128)(2,1)}), bf16[512,64,128]{2,1,0:T(8,128)(2,1)}) %all-gather.6.cloned.1.call-update) | async-done | bytes 8388624 | tf_op jit(solution)/shard_map/all_gather | solution.py:238
  83.0 8.1 %pick.1 = f32[8,32768]{1,0:T(8,128)} custom-call(bf16[8,128]{1,0:T(8,128)(2,1)} %compare_convert_fusion.onehot_ref, bf16[4,128,64,128]{3,2,1,0:T(8,128)(2,1)} %bitcast.8), custom_call_target="tpu_custom_call" | custom-call | tf_op jit(solution)/shard_map/pick/pallas_call | solution.py:127
  91.1 1.3 convert.6
  92.3 0.8 pad_maximum_fusion
  93.2 0.0 all-gather.4.cloned.1.call-update
  93.2 0.6 pad_bitcast_fusion.qual_ref
  93.8 73.1 %all-gather.4.cloned.1.call-done.src_ref.flags_ref = bf16[64,32896]{1,0:T(8,128)(2,1)} async-done(((bf16[8,32896]{1,0:T(8,128)(2,1)}), bf16[64,32896]{1,0:T(8,128)(2,1)}) %all-gather.4.cloned.1.call-update) | async-done | bytes 4210704 | tf_op jit(solution)/shard_map/all_gather | solution.py:247
  166.9 77.2 %correlate.1 = f32[64,201,128]{2,1,0:T(8,128)} custom-call(bf16[4,128,64,128]{3,2,1,0:T(8,128)(2,1)} %bitcast.9, bf16[64,32896]{1,0:T(8,128)(2,1)} %all-gather.4.cloned.1.call-done.src_ref.flags_ref, bf16[64,32896]{1,0:T(8,128)(2,1)} %all-gather.4.cloned.1.call-done.src_ref.flags_ref, bf16[128,128]{1,0:T(8,128)(2,1)} %pad_bitcast_fusion.qual_ref, ...), custom_call_target="tpu_custom_call" | custom-call | flops 15569256448 | bytes 40000000 | tf_op jit(solution)/shard_map/correlate/pallas_call | solution.py:210
  244.1 7.9 %copy.11 = f32[64,201,128]{2,0,1:T(8,128)} copy(f32[64,201,128]{2,1,0:T(8,128)} %correlate.1) | data formatting | bytes 13172736 | tf_op jit(solution)/shard_map/correlate/pallas_call | solution.py:210
  (2 shorter events, 0.0 us)
Async XLA Ops:
  6.5 3.9 %copy-start = (s32[128,16]{0,1:T(8,128)S(1)}, s32[128,16]{0,1:T(8,128)}, u32[]{:S(2)}) copy-start(s32[128,16]{0,1:T(8,128)} %param.7) | copy-start | bytes 24580
  6.5 76.4 %all-gather.6.cloned.1.call-start = ((), (), s32[]{:S(2)}) async-start(), calls=%async_computation.1 | async-start | bytes 10485760 | tf_op jit(solution)/shard_map/all_gather | solution.py:238
  21.8 0.7 copy-start.1
  21.8 145.1 %all-gather.4.cloned.1.call-start = ((), (), s32[]{:S(2)}) async-start(), calls=%async_computation | async-start | bytes 4737024 | tf_op jit(solution)/shard_map/all_gather | solution.py:247
Sparse Core Ops, SparseCore 0:
  21.9 60.9 all-gather.5
  93.3 73.5 all-gather.3

commit v2 on v1

v2 whole, which is shorter than its diff:
```python
import functools
import math

import jax
import jax.numpy as jnp
import ml_dtypes
import numpy as np
from jax import lax
from jax.experimental import pallas as pl
from jax.experimental.pallas import tpu as pltpu
from jax.sharding import PartitionSpec as P

LAGH = 100
BINS = 8
GROUPS_STEP = 16
VMEM = 60 * 1024 * 1024


def padded_groups(length):
    groups = -(-(length // 2 + 1) // BINS)
    return -(-groups // GROUPS_STEP) * GROUPS_STEP


def make_tables(length):
    half = length // 2
    pad = padded_groups(length) * BINS
    bins = np.arange(1, half + 1)
    unit = np.float32(2.0 * math.pi / length)
    phase = (bins[:, None] * np.arange(length)[None, :] % length).astype(np.float32) * unit
    forward = np.zeros((2, pad, length), np.float32)
    forward[0, :half] = np.cos(phase)
    forward[1, :half] = -np.sin(phase)
    lags = np.arange(-LAGH, LAGH + 1)
    phase = (lags[:, None] * bins[None, :] % length).astype(np.float32) * unit
    weights = np.where(bins == half, 1.0, 2.0).astype(np.float32) / np.sqrt(np.float32(half))
    nlag = 2 * LAGH + 1
    inverse = np.zeros((-(-nlag // 16) * 16, 2, pad), np.float32)
    inverse[:nlag, 0, :half] = weights * np.cos(phase)
    inverse[:nlag, 1, :half] = -weights * np.sin(phase)
    step = GROUPS_STEP * BINS
    inverse[nlag, 0, half] = 1.0
    inverse = inverse.reshape(-1, 2, pad // step, step).transpose(2, 0, 1, 3)
    inverse = inverse.reshape(pad // step, -1, 2 * step)
    return forward.astype(ml_dtypes.bfloat16), inverse.astype(ml_dtypes.bfloat16)


def whiten_kernel(half, seg, forward_ref, traces_ref, quality_ref, out_ref, spec, power):
    step = pl.program_id(0)
    rows = forward_ref.shape[1]
    cols = traces_ref.shape[0]
    width = cols // seg
    part = lax.dot_general(
        forward_ref[...].reshape(2 * rows, -1),
        traces_ref[...],
        (((1,), (1,)), ((), ())),
        preferred_element_type=jnp.float32,
    )
    re, im = part[:rows], part[rows:]
    start = pl.multiple_of(step * rows, rows)
    spec[0, pl.ds(start, rows), :] = re
    spec[1, pl.ds(start, rows), :] = im
    total = jnp.sum((re * re + im * im).reshape(rows // 8, 8, cols), axis=0)

    @pl.when(step == 0)
    def _():
        power[...] = total

    @pl.when(step > 0)
    def _():
        power[...] += total

    @pl.when(step == pl.num_programs(0) - 1)
    def _():
        mean = jnp.sum(power[...], axis=0, keepdims=True) * (1.0 / half)
        level = 0.5 * jnp.sqrt(mean + 1e-06)
        qual = quality_ref[...]

        def one_group(g, carry):
            at = pl.ds(pl.multiple_of(g * BINS, BINS), BINS)
            re, im = spec[0, at, :], spec[1, at, :]
            scale = qual / jnp.maximum(jnp.sqrt(re * re + im * im), level)
            parts = []
            for value in (re * scale, im * scale):
                for s in range(seg):
                    parts.append(value[:, s * width : (s + 1) * width])
            out_ref[g] = jnp.concatenate(parts, axis=0).astype(jnp.bfloat16)
            return carry

        lax.fori_loop(0, half // BINS, one_group, 0, unroll=5)
        first = lax.broadcasted_iota(jnp.int32, (BINS, width), 0) == 0
        parts = [jnp.where(first, qual[:, s * width : (s + 1) * width], 0.0) for s in range(seg)]
        parts += [jnp.zeros_like(part) for part in parts]
        out_ref[half // BINS] = jnp.concatenate(parts, axis=0).astype(jnp.bfloat16)
        for g in range(half // BINS + 1, out_ref.shape[0]):
            out_ref[g] = jnp.zeros(out_ref.shape[1:], jnp.bfloat16)


def whiten(traces, quality_local, forward):
    rows, seg, length = traces.shape
    pad = forward.shape[1]
    steps = 4
    cols = rows * seg
    return pl.pallas_call(
        functools.partial(whiten_kernel, length // 2, seg),
        grid=(steps,),
        in_specs=[
            pl.BlockSpec((2, pad // steps, length), lambda i: (0, i, 0)),
            pl.BlockSpec((cols, length), lambda i: (0, 0)),
            pl.BlockSpec((1, cols), lambda i: (0, 0)),
        ],
        out_specs=pl.BlockSpec((pad // BINS, 2 * seg * BINS, rows), lambda i: (0, 0, 0)),
        out_shape=jax.ShapeDtypeStruct((pad // BINS, 2 * seg * BINS, rows), jnp.bfloat16),
        scratch_shapes=[
            pltpu.VMEM((2, pad, cols), jnp.float32),
            pltpu.VMEM((8, cols), jnp.float32),
        ],
        compiler_params=pltpu.CompilerParams(vmem_limit_bytes=VMEM),
        name="whiten",
    )(forward, traces.transpose(1, 0, 2).reshape(cols, length), quality_local)


def other(a, bit):
    low, high = a % 2, a // 2
    return high * 2 + 1 - low if bit == 0 else (1 - high) * 2 + low


def stack_kernel(
    blocks, white_ref, onehot_ref, inverse_ref, out_ref,
    ybuf, xbuf, cross, acc, own_sem, y_send, y_recv, z_send, z_recv, p_send, p_recv,
):
    parts, _, depth, width = ybuf.shape
    full = parts * depth
    _, chunks, rows16, lanes = xbuf.shape
    groups = GROUPS_STEP
    rep = groups * full // lanes
    each = rows16 // rep
    nsrc = each * blocks
    outer = blocks // 2
    nlag = out_ref.shape[0] // nsrc
    half_k = groups * BINS
    a, b = lax.axis_index("src"), lax.axis_index("rcv")
    core, far = other(a, 0), other(a, 1)
    diag = other(far, 0)
    line, side = b // 2, b % 2
    mate = line * 2 + 1 - side

    barrier = pltpu.get_barrier_semaphore()
    peers = [{"src": core}, {"src": far}, {"rcv": mate}]
    peers += [{"rcv": ((line + d) % outer) * 2 + side} for d in range(1, outer)]
    for peer in peers:
        pl.semaphore_signal(barrier, inc=1, device_id=peer, device_id_type=pl.DeviceIdType.MESH)
    pl.semaphore_wait(barrier, len(peers))

    def groups_of(c):
        return pl.ds(c * groups, groups)

    def own_copy():
        return pltpu.make_async_copy(white_ref, ybuf.at[a], own_sem)

    def send(src, dst, send_sem, recv_sem, device):
        return pltpu.make_async_remote_copy(
            src_ref=src, dst_ref=dst, send_sem=send_sem, recv_sem=recv_sem,
            device_id=device, device_id_type=pl.DeviceIdType.MESH,
        )

    def y_copy(c, kind):
        at = groups_of(c)
        if kind == 2:
            src, dst = ybuf.at[far, at], ybuf.at[far, at]
        else:
            src, dst = white_ref.at[at], ybuf.at[a, at]
        return send(
            src, dst, y_send.at[c, kind], y_recv.at[c, kind], {"src": far if kind == 0 else core}
        )

    def y_wait(c, kind):
        at = groups_of(c)
        got = (far, core, diag)[kind]
        send(
            ybuf.at[got, at], ybuf.at[got, at], y_send.at[c, kind], y_recv.at[c, kind],
            {"src": far if kind == 0 else core},
        ).wait_recv()

    def z_copy(c, d):
        there = ((line + d) % outer) * 2 + side
        return send(xbuf.at[b, c], xbuf.at[b, c], z_send.at[c, d], z_recv.at[c, d], {"rcv": there})

    def z_wait(c, d):
        start = ((line + outer - d) % outer) * 2 + side
        send(
            xbuf.at[start, c], xbuf.at[start, c], z_send.at[c, d], z_recv.at[c, d], {"rcv": start}
        ).wait_recv()

    def p_copy(c, d):
        start = ((line + outer - d) % outer) * 2 + side
        return send(
            xbuf.at[start, c], xbuf.at[start, c], p_send.at[c, d], p_recv.at[c, d], {"rcv": mate}
        )

    def p_wait(c, d):
        start = ((line + outer - d) % outer) * 2 + 1 - side
        send(
            xbuf.at[start, c], xbuf.at[start, c], p_send.at[c, d], p_recv.at[c, d], {"rcv": mate}
        ).wait_recv()

    def start_own(c, carry):
        y_copy(c, 0).start()
        y_copy(c, 1).start()
        return carry

    lax.fori_loop(0, chunks, start_own, 0)
    own_copy().start()
    acc[...] = jnp.zeros_like(acc)
    own_copy().wait()

    row16 = lax.broadcasted_iota(jnp.int32, (rows16, full), 0)
    lane = lax.broadcasted_iota(jnp.int32, (1, BINS, full), 2)
    row = lax.broadcasted_iota(jnp.int32, (1, BINS, full), 1)
    mask = lane % BINS == row

    def pick(c):
        for t in range(groups // rep):
            found = None
            for sub in range(rep):
                block = ybuf[:, c * groups + t * rep + sub].reshape(full, width)
                part = lax.dot_general(
                    onehot_ref[...], block, (((1,), (1,)), ((), ())),
                    preferred_element_type=jnp.float32,
                )
                found = part if sub == 0 else jnp.where(row16 // each == sub, part, found)
            xbuf[b, c, :, t * full : (t + 1) * full] = found.astype(jnp.bfloat16)

    def multiply(c):
        def one_step(t, carry):
            x_all = xbuf[:, c, :, pl.ds(pl.multiple_of(t * full, full), full)].astype(jnp.float32)
            for s0 in range(0, rep, 2):
                products = []
                for sub in (s0, s0 + 1):
                    y = ybuf[:, c * groups + t * rep + sub].reshape(parts, 2, depth // 2, width)
                    turned = jnp.concatenate([-y[:, 1:], y[:, :1]], axis=1)
                    right = jnp.concatenate(
                        [y.reshape(full, width), turned.reshape(full, width)], axis=1
                    )
                    left = []
                    for n in range(each):
                        r = sub * each + n
                        left.append(jnp.where(mask, x_all[:, r : r + 1, :], 0.0))
                    left = jnp.concatenate(left, axis=0).reshape(nsrc * BINS, full)
                    prod = jnp.dot(
                        left.astype(jnp.bfloat16), right, preferred_element_type=jnp.float32
                    )
                    products.append(prod.reshape(nsrc, BINS, 2 * width))
                both = jnp.concatenate(products, axis=1).astype(jnp.bfloat16)
                at = pl.multiple_of((t * rep + s0) * BINS, 2 * BINS)
                cross[:, pl.ds(at, 2 * BINS), :] = both[:, :, :width]
                cross[:, pl.ds(half_k + at, 2 * BINS), :] = both[:, :, width:]
            return carry

        lax.fori_loop(0, groups // rep, one_step, 0, unroll=2)

    def invert(c):
        table = inverse_ref[c]

        def add_pair(p, carry):
            right = jnp.concatenate([cross[2 * p], cross[2 * p + 1]], axis=1)
            lagged = jnp.dot(table, right, preferred_element_type=jnp.float32)
            acc[2 * p] += lagged[:, :width]
            acc[2 * p + 1] += lagged[:, width:]
            return carry

        lax.fori_loop(0, nsrc // 2, add_pair, 0, unroll=4)

    def one_chunk(c, carry):
        @pl.when(c < chunks)
        def _():
            y_wait(c, 0)
            y_copy(c, 2).start()

        @pl.when(jnp.logical_and(c >= 1, c <= chunks))
        def _():
            y_wait(c - 1, 1)
            y_wait(c - 1, 2)
            pick(c - 1)
            for d in range(1, outer):
                z_copy(c - 1, d).start()
            p_copy(c - 1, 0).start()

        @pl.when(jnp.logical_and(c >= 2, c <= chunks + 1))
        def _():
            for d in range(1, outer):
                z_wait(c - 2, d)
                p_copy(c - 2, d).start()

        @pl.when(c >= 3)
        def _():
            for d in range(outer):
                p_wait(c - 3, d)
            multiply(c - 3)
            invert(c - 3)

        return carry

    lax.fori_loop(0, chunks + 3, one_chunk, 0)

    def finish(i, carry):
        value = acc[i]
        scale = 1.0 / jnp.maximum(value[nlag : nlag + 1], 1.0)
        out_ref[pl.ds(i, nlag, stride=nsrc), :] = value[:nlag] * scale
        return carry

    lax.fori_loop(0, nsrc, finish, 0)

    def drain(c, carry):
        for kind in range(3):
            y_copy(c, kind).wait_send()
        for d in range(1, outer):
            z_copy(c, d).wait_send()
        for d in range(outer):
            p_copy(c, d).wait_send()
        return carry

    lax.fori_loop(0, chunks, drain, 0)


def stack(white, onehot, inverse, parts, blocks):
    total, depth, rows = white.shape
    chunks, taps, depth_k = inverse.shape
    nlag = 2 * LAGH + 1
    nsrc = blocks * onehot.shape[0]
    rep = 16 // onehot.shape[0]
    lanes = GROUPS_STEP * parts * depth // rep
    outer = blocks // 2
    flops = 2 * nsrc * rows * total * (BINS * parts * depth * 2 + 2 * BINS * taps)
    return pl.pallas_call(
        functools.partial(stack_kernel, blocks),
        in_specs=[
            pl.BlockSpec(memory_space=pl.ANY),
            pl.BlockSpec(memory_space=pltpu.VMEM),
            pl.BlockSpec(memory_space=pltpu.VMEM),
        ],
        out_specs=pl.BlockSpec(memory_space=pltpu.VMEM),
        out_shape=jax.ShapeDtypeStruct((nlag * nsrc, rows), jnp.float32),
        scratch_shapes=[
            pltpu.VMEM((parts, total, depth, rows), jnp.bfloat16),
            pltpu.VMEM((blocks, chunks, 16, lanes), jnp.bfloat16),
            pltpu.VMEM((nsrc, depth_k, rows), jnp.bfloat16),
            pltpu.VMEM((nsrc, taps, rows), jnp.float32),
            pltpu.SemaphoreType.DMA,
            pltpu.SemaphoreType.DMA((chunks, 3)),
            pltpu.SemaphoreType.DMA((chunks, 3)),
            pltpu.SemaphoreType.DMA((chunks, outer)),
            pltpu.SemaphoreType.DMA((chunks, outer)),
            pltpu.SemaphoreType.DMA((chunks, outer)),
            pltpu.SemaphoreType.DMA((chunks, outer)),
        ],
        compiler_params=pltpu.CompilerParams(
            vmem_limit_bytes=VMEM, collective_id=0, has_side_effects=True
        ),
        cost_estimate=pl.CostEstimate(flops=flops, bytes_accessed=20_000_000, transcendentals=0),
        name="stack",
    )(white, jnp.tile(onehot, (rep, 1)), inverse)


def on_device(parts, blocks, traces, src_index, quality):
    rows, seg_local, length = traces.shape
    nsrc = src_index.shape[0]
    each = nsrc // blocks
    forward, inverse = make_tables(length)
    here, part = lax.axis_index("rcv"), lax.axis_index("src")
    mine = lax.dynamic_slice_in_dim(quality, part * seg_local, seg_local, axis=1)
    mine = mine.astype(jnp.float32).T.reshape(1, rows * seg_local)
    white = whiten(traces, mine, jnp.asarray(forward))
    own = lax.dynamic_index_in_dim(src_index.reshape(each, blocks), here, 1, keepdims=False)
    onehot = (own[:, None] == here * rows + jnp.arange(rows, dtype=jnp.int32)[None, :]).astype(
        jnp.bfloat16
    )
    out = stack(white, onehot, jnp.asarray(inverse), parts, blocks)
    return out.reshape(2 * LAGH + 1, nsrc, rows).transpose(1, 0, 2)


def solution(mesh):
    return jax.shard_map(
        functools.partial(on_device, mesh.shape["src"], mesh.shape["rcv"]),
        mesh=mesh,
        in_specs=(P("rcv", "src", None), P("src"), P("rcv", None)),
        out_specs=P("src", None, "rcv"),
        check_vma=False,
    )
```

time: 259 us -> 113 us (0.44)
  waiting for transfers between devices: 133 us -> 0 us
  between operations: 13.4 us -> 0.01 us
  Pallas kernels: 96 us -> 98.6 us
    all_gather x2 -> x0, waiting for transfers between devices: 133 us -> none  [the longest x1 73.1 us: on_device(): got = lax.all_gather(sent, 'rcv', axis=0, tiled=True)]
    pallas_call x1 -> x0, local copies, waits for them, and re-layouts: 7.85 us -> none  [correlate(): pl.pallas_call(functools.partial(correlate_kernel, blocks), grid=(groups...]
    unnamed x4 -> x1, local copies, waits for them, and re-layouts: 0.57 us -> 6.87 us
    pallas_call x2 -> x1, Pallas kernels: 85.3 us -> 88 us  [stack(): pl.pallas_call(functools.partial(stack_kernel, blocks), in_specs=[pl.Bloc...]
  transfers between devices with their start and end apart: 2 -> 0, of which waited for: 2 -> 0; matrix products, arithmetic and copies ran while one was open for 1% -> 0% of each run, Pallas kernels for 0% -> 0%
where the time goes in v2:
time: 113 us; the launch traced here: 112 us
  Pallas kernels  98.6 us (87%)
  local copies, waits for them, and re-layouts  12.3 us (11%)
  other arithmetic  1.36 us (1%)
    pallas_call x1, Pallas kernels, stack(): pl.pallas_call(functools.partial(stack_kernel, blocks), in_specs=[pl.Bloc...  88 us
    pallas_call x1, Pallas kernels, whiten(): pl.pallas_call(functools.partial(whiten_kernel, length // 2, seg), grid=(...  10.6 us
    unnamed x1, local copies, waits for them, and re-layouts  6.87 us
    transpose x1, local copies, waits for them, and re-layouts, whiten(): traces.transpose(1, 0, 2).reshape(cols, length)  3.87 us

profile of v2, /device:TPU:0, one launch (start us, length us, event | category | flops | bytes accessed | tf_op | source)
XLA Modules:
  0.0 112.2 jit_solution(17433826654486129760)
XLA Ops:
  0.0 1.3 %dynamic-slice_convert_fusion = f32[128,4]{0,1:T(4,128)} fusion(s32[128,16]{0,1:T(8,128)} %param.7, s32[]{:T(128)S(6)} %select_n.7), kind=kLoop, calls=%fused_computation.3 | loop fusion | flops 512 | bytes 4100 | tf_op jit(solution)/shard_map/convert_element_type | solution.py:371
  1.3 0.7 reshape.50
  2.0 0.2 dynamic-slice_reduce_fusion
  2.2 0.1 compare_convert_fusion
  2.3 0.6 broadcast_bitcast_fusion.onehot_ref
  2.9 3.9 %copy.7 = bf16[4,128,2000]{2,1,0:T(8,128)(2,1)} copy(bf16[4,128,2000]{1,2,0:T(8,128)(2,1)} %bitcast.12) | data formatting | bytes 4096000 | tf_op jit(solution)/shard_map/transpose | solution.py:119
  6.8 10.6 %whiten.1.white_ref = bf16[128,64,128]{2,1,0:T(8,128)(2,1)} custom-call(bf16[2,1024,2000]{2,1,0:T(8,128)(2,1)} %constant.25.clone.forward_ref, bf16[512,2000]{1,0:T(8,128)(2,1)} %bitcast.10, f32[1,512]{1,0:T(1,128)} %bitcast.13), custom_call_target="tpu_custom_call" | custom-call | tf_op jit(solution)/shard_map/whiten/pallas_call | solution.py:103
  17.3 88.0 %stack.1 = f32[12864,128]{1,0:T(8,128)} custom-call(bf16[128,64,128]{2,1,0:T(8,128)(2,1)} %whiten.1.white_ref, bf16[16,128]{1,0:T(8,128)(2,1)} %broadcast_bitcast_fusion.onehot_ref, bf16[8,208,256]{2,1,0:T(8,128)(2,1)} %constant.26.clone.inverse_ref), custom_call_target="tpu_custom_call" | custom-call | flops 15569256448 | bytes 20000000 | tf_op jit(solution)/shard_map/stack/pallas_call | solution.py:334
  105.4 6.9 %copy.9 = f32[64,201,128]{2,0,1:T(8,128)} copy(f32[64,201,128]{2,0,1:T(8,128)} %bitcast.11) | data formatting | bytes 13172736
  (1 shorter events, 0.0 us)

commit v3 on v2

--- a/solution.py
+++ b/solution.py
@@ -13,12 +13,13 @@
 LAGH = 100
 BINS = 8
 GROUPS_STEP = 16
+INVERT = 2
 VMEM = 60 * 1024 * 1024
 
 
 def padded_groups(length):
     groups = -(-(length // 2 + 1) // BINS)
-    return -(-groups // GROUPS_STEP) * GROUPS_STEP
+    return -(-groups // (GROUPS_STEP * INVERT)) * GROUPS_STEP * INVERT
 
 
 def make_tables(length):
@@ -39,20 +40,20 @@
     inverse[:nlag, 1, :half] = -weights * np.sin(phase)
     step = GROUPS_STEP * BINS
     inverse[nlag, 0, half] = 1.0
-    inverse = inverse.reshape(-1, 2, pad // step, step).transpose(2, 0, 1, 3)
-    inverse = inverse.reshape(pad // step, -1, 2 * step)
+    inverse = inverse.reshape(-1, 2, pad // step // INVERT, INVERT, step).transpose(2, 0, 3, 1, 4)
+    inverse = inverse.reshape(pad // step // INVERT, -1, INVERT * 2 * step)
     return forward.astype(ml_dtypes.bfloat16), inverse.astype(ml_dtypes.bfloat16)
 
 
 def whiten_kernel(half, seg, forward_ref, traces_ref, quality_ref, out_ref, spec, power):
     step = pl.program_id(0)
     rows = forward_ref.shape[1]
-    cols = traces_ref.shape[0]
-    width = cols // seg
+    width = traces_ref.shape[2]
+    cols = seg * width
     part = lax.dot_general(
         forward_ref[...].reshape(2 * rows, -1),
-        traces_ref[...],
-        (((1,), (1,)), ((), ())),
+        jnp.concatenate([traces_ref[s] for s in range(seg)], axis=1),
+        (((1,), (0,)), ((), ())),
         preferred_element_type=jnp.float32,
     )
     re, im = part[:rows], part[rows:]
@@ -105,7 +106,7 @@
         grid=(steps,),
         in_specs=[
             pl.BlockSpec((2, pad // steps, length), lambda i: (0, i, 0)),
-            pl.BlockSpec((cols, length), lambda i: (0, 0)),
+            pl.BlockSpec((seg, length, rows), lambda i: (0, 0, 0)),
             pl.BlockSpec((1, cols), lambda i: (0, 0)),
         ],
         out_specs=pl.BlockSpec((pad // BINS, 2 * seg * BINS, rows), lambda i: (0, 0, 0)),
@@ -116,7 +117,7 @@
         ],
         compiler_params=pltpu.CompilerParams(vmem_limit_bytes=VMEM),
         name="whiten",
-    )(forward, traces.transpose(1, 0, 2).reshape(cols, length), quality_local)
+    )(forward, traces.transpose(1, 2, 0), quality_local)
 
 
 def other(a, bit):
@@ -125,8 +126,8 @@
 
 
 def stack_kernel(
-    blocks, white_ref, onehot_ref, inverse_ref, out_ref,
-    ybuf, xbuf, cross, acc, own_sem, y_send, y_recv, z_send, z_recv, p_send, p_recv,
+    blocks, white_ref, onehot_ref, inverse_ref, acc,
+    ybuf, xbuf, xf, cross, own_sem, y_send, y_recv, z_send, z_recv, p_send, p_recv,
 ):
     parts, _, depth, width = ybuf.shape
     full = parts * depth
@@ -136,7 +137,6 @@
     each = rows16 // rep
     nsrc = each * blocks
     outer = blocks // 2
-    nlag = out_ref.shape[0] // nsrc
     half_k = groups * BINS
     a, b = lax.axis_index("src"), lax.axis_index("rcv")
     core, far = other(a, 0), other(a, 1)
@@ -214,8 +214,8 @@
     own_copy().wait()
 
     row16 = lax.broadcasted_iota(jnp.int32, (rows16, full), 0)
-    lane = lax.broadcasted_iota(jnp.int32, (1, BINS, full), 2)
-    row = lax.broadcasted_iota(jnp.int32, (1, BINS, full), 1)
+    lane = lax.broadcasted_iota(jnp.int32, (BINS, full), 1)
+    row = lax.broadcasted_iota(jnp.int32, (BINS, full), 0)
     mask = lane % BINS == row
 
     def pick(c):
@@ -231,8 +231,10 @@
             xbuf[b, c, :, t * full : (t + 1) * full] = found.astype(jnp.bfloat16)
 
     def multiply(c):
+        xf[...] = xbuf[:, c].astype(jnp.float32)
+
         def one_step(t, carry):
-            x_all = xbuf[:, c, :, pl.ds(pl.multiple_of(t * full, full), full)].astype(jnp.float32)
+            cols = pl.ds(pl.multiple_of(t * full, full), full)
             for s0 in range(0, rep, 2):
                 products = []
                 for sub in (s0, s0 + 1):
@@ -244,14 +246,15 @@
                     left = []
                     for n in range(each):
                         r = sub * each + n
-                        left.append(jnp.where(mask, x_all[:, r : r + 1, :], 0.0))
-                    left = jnp.concatenate(left, axis=0).reshape(nsrc * BINS, full)
+                        for k in range(blocks):
+                            left.append(jnp.where(mask, xf[k, r : r + 1, cols], 0.0))
+                    left = jnp.concatenate(left, axis=0)
                     prod = jnp.dot(
                         left.astype(jnp.bfloat16), right, preferred_element_type=jnp.float32
                     )
                     products.append(prod.reshape(nsrc, BINS, 2 * width))
                 both = jnp.concatenate(products, axis=1).astype(jnp.bfloat16)
-                at = pl.multiple_of((t * rep + s0) * BINS, 2 * BINS)
+                at = pl.multiple_of(c % INVERT * 2 * half_k + (t * rep + s0) * BINS, 2 * BINS)
                 cross[:, pl.ds(at, 2 * BINS), :] = both[:, :, :width]
                 cross[:, pl.ds(half_k + at, 2 * BINS), :] = both[:, :, width:]
             return carry
@@ -259,7 +262,7 @@
         lax.fori_loop(0, groups // rep, one_step, 0, unroll=2)
 
     def invert(c):
-        table = inverse_ref[c]
+        table = inverse_ref[c // INVERT]
 
         def add_pair(p, carry):
             right = jnp.concatenate([cross[2 * p], cross[2 * p + 1]], axis=1)
@@ -296,19 +299,14 @@
             for d in range(outer):
                 p_wait(c - 3, d)
             multiply(c - 3)
-            invert(c - 3)
+
+            @pl.when((c - 3) % INVERT == INVERT - 1)
+            def _():
+                invert(c - 3)
 
         return carry
 
     lax.fori_loop(0, chunks + 3, one_chunk, 0)
-
-    def finish(i, carry):
-        value = acc[i]
-        scale = 1.0 / jnp.maximum(value[nlag : nlag + 1], 1.0)
-        out_ref[pl.ds(i, nlag, stride=nsrc), :] = value[:nlag] * scale
-        return carry
-
-    lax.fori_loop(0, nsrc, finish, 0)
 
     def drain(c, carry):
         for kind in range(3):
@@ -324,8 +322,8 @@
 
 def stack(white, onehot, inverse, parts, blocks):
     total, depth, rows = white.shape
-    chunks, taps, depth_k = inverse.shape
-    nlag = 2 * LAGH + 1
+    steps, taps, depth_k = inverse.shape
+    chunks = steps * INVERT
     nsrc = blocks * onehot.shape[0]
     rep = 16 // onehot.shape[0]
     lanes = GROUPS_STEP * parts * depth // rep
@@ -339,12 +337,12 @@
             pl.BlockSpec(memory_space=pltpu.VMEM),
         ],
         out_specs=pl.BlockSpec(memory_space=pltpu.VMEM),
-        out_shape=jax.ShapeDtypeStruct((nlag * nsrc, rows), jnp.float32),
+        out_shape=jax.ShapeDtypeStruct((nsrc, taps, rows), jnp.float32),
         scratch_shapes=[
             pltpu.VMEM((parts, total, depth, rows), jnp.bfloat16),
             pltpu.VMEM((blocks, chunks, 16, lanes), jnp.bfloat16),
+            pltpu.VMEM((blocks, 16, lanes), jnp.float32),
             pltpu.VMEM((nsrc, depth_k, rows), jnp.bfloat16),
-            pltpu.VMEM((nsrc, taps, rows), jnp.float32),
             pltpu.SemaphoreType.DMA,
             pltpu.SemaphoreType.DMA((chunks, 3)),
             pltpu.SemaphoreType.DMA((chunks, 3)),
@@ -361,21 +359,40 @@
     )(white, jnp.tile(onehot, (rep, 1)), inverse)
 
 
+def finish_kernel(acc_ref, out_ref):
+    nlag = out_ref.shape[0]
+    for n in range(acc_ref.shape[0]):
+        count = acc_ref[n, nlag : nlag + 1, :]
+        out_ref[:, n, :] = acc_ref[n, :nlag, :] * (1.0 / jnp.maximum(count, 1.0))
+
+
+def finish(acc):
+    nsrc, taps, rows = acc.shape
+    nlag, tile = 2 * LAGH + 1, 8
+    return pl.pallas_call(
+        finish_kernel,
+        grid=(nsrc // tile,),
+        in_specs=[pl.BlockSpec((tile, taps, rows), lambda i: (i, 0, 0))],
+        out_specs=pl.BlockSpec((nlag, tile, rows), lambda i: (0, i, 0)),
+        out_shape=jax.ShapeDtypeStruct((nlag, nsrc, rows), jnp.float32),
+        name="finish",
+    )(acc)
+
+
 def on_device(parts, blocks, traces, src_index, quality):
     rows, seg_local, length = traces.shape
     nsrc = src_index.shape[0]
     each = nsrc // blocks
     forward, inverse = make_tables(length)
     here, part = lax.axis_index("rcv"), lax.axis_index("src")
-    mine = lax.dynamic_slice_in_dim(quality, part * seg_local, seg_local, axis=1)
-    mine = mine.astype(jnp.float32).T.reshape(1, rows * seg_local)
+    mine = lax.dynamic_slice_in_dim(quality.T, part * seg_local, seg_local, axis=0)
+    mine = mine.astype(jnp.float32).reshape(1, rows * seg_local)
     white = whiten(traces, mine, jnp.asarray(forward))
     own = lax.dynamic_index_in_dim(src_index.reshape(each, blocks), here, 1, keepdims=False)
     onehot = (own[:, None] == here * rows + jnp.arange(rows, dtype=jnp.int32)[None, :]).astype(
         jnp.bfloat16
     )
-    out = stack(white, onehot, jnp.asarray(inverse), parts, blocks)
-    return out.reshape(2 * LAGH + 1, nsrc, rows).transpose(1, 0, 2)
+    return finish(stack(white, onehot, jnp.asarray(inverse), parts, blocks)).transpose(1, 0, 2)
 
 
 def solution(mesh):

time: 113 us -> 106 us (0.938)
  local copies, waits for them, and re-layouts: 12.3 us -> 1.52 us
  Pallas kernels: 98.6 us -> 103 us
    pallas_call x0 -> x1, Pallas kernels: none -> 9.21 us  [finish(): pl.pallas_call(finish_kernel, grid=(nsrc // tile,), in_specs=[pl.BlockSpe...]
    unnamed x1 -> x0, local copies, waits for them, and re-layouts: 6.87 us -> none
    pallas_call x1, Pallas kernels: 88 us -> 83.2 us  [stack(): pl.pallas_call(functools.partial(stack_kernel, blocks), in_specs=[pl.Bloc...]
    transpose x1 -> x0, local copies, waits for them, and re-layouts: 3.87 us -> none  [whiten(): traces.transpose(1, 0, 2).reshape(cols, length)]
where the time goes in v3:
time: 106 us
  Pallas kernels  103 us (97%)
  local copies, waits for them, and re-layouts  1.52 us (1%)
  other arithmetic  1.36 us (1%)
    pallas_call x1, Pallas kernels, stack(): pl.pallas_call(functools.partial(stack_kernel, blocks), in_specs=[pl.Bloc...  83.2 us
    pallas_call x1, Pallas kernels, whiten(): pl.pallas_call(functools.partial(whiten_kernel, length // 2, seg), grid=(...  10.4 us
    pallas_call x1, Pallas kernels, finish(): pl.pallas_call(finish_kernel, grid=(nsrc // tile,), in_specs=[pl.BlockSpe...  9.21 us

profile of v3, /device:TPU:0, one launch (start us, length us, event | category | flops | bytes accessed | tf_op | source)
XLA Modules:
  0.0 105.8 jit_solution(12464995186518678136)
XLA Ops:
  0.0 1.3 %dynamic-slice_convert_fusion = f32[128,4]{0,1:T(4,128)} fusion(s32[128,16]{0,1:T(8,128)} %param.7, s32[]{:T(128)S(6)} %select_n.7), kind=kLoop, calls=%fused_computation.3 | loop fusion | flops 512 | bytes 4100 | tf_op jit(solution)/shard_map/convert_element_type | solution.py:389
  1.3 0.7 reshape.43
  2.0 0.2 dynamic-slice_reduce_fusion
  2.2 0.1 compare_convert_fusion
  2.3 0.6 broadcast_bitcast_fusion.onehot_ref
  2.9 10.4 %whiten.1.white_ref = bf16[128,64,128]{2,1,0:T(8,128)(2,1)} custom-call(bf16[2,1024,2000]{2,1,0:T(8,128)(2,1)} %constant.25.clone.forward_ref, bf16[4,2000,128]{2,1,0:T(8,128)(2,1)} %bitcast.7, f32[1,512]{1,0:T(1,128)} %bitcast.8), custom_call_target="tpu_custom_call" | custom-call | tf_op jit(solution)/shard_map/whiten/pallas_call | solution.py:104
  13.3 83.2 %stack.1.acc_ref = f32[64,208,128]{2,1,0:T(8,128)} custom-call(bf16[128,64,128]{2,1,0:T(8,128)(2,1)} %whiten.1.white_ref, bf16[16,128]{1,0:T(8,128)(2,1)} %broadcast_bitcast_fusion.onehot_ref, bf16[4,208,512]{2,1,0:T(8,128)(2,1)} %constant.26.clone.inverse_ref), custom_call_target="tpu_custom_call" | custom-call | flops 15569256448 | bytes 20000000 | tf_op jit(solution)/shard_map/stack/pallas_call | solution.py:332
  96.6 9.2 %finish.1 = f32[201,64,128]{2,1,0:T(8,128)} custom-call(f32[64,208,128]{2,1,0:T(8,128)} %stack.1.acc_ref), custom_call_target="tpu_custom_call" | custom-call | tf_op jit(solution)/shard_map/finish/pallas_call | solution.py:372
  (1 shorter events, 0.0 us)

commit v4 on v3

--- a/solution.py
+++ b/solution.py
@@ -12,8 +12,9 @@
 
 LAGH = 100
 BINS = 8
-GROUPS_STEP = 16
-INVERT = 2
+GROUPS_STEP = 8
+INVERT = 4
+AHEAD = 4
 VMEM = 60 * 1024 * 1024
 
 
@@ -74,7 +75,10 @@
     def _():
         mean = jnp.sum(power[...], axis=0, keepdims=True) * (1.0 / half)
         level = 0.5 * jnp.sqrt(mean + 1e-06)
-        qual = quality_ref[...]
+        first_row = lax.axis_index("src") * seg
+        qual = jnp.concatenate(
+            [quality_ref[pl.ds(first_row + s, 1), :] for s in range(seg)], axis=1
+        ).astype(jnp.float32)
 
         def one_group(g, carry):
             at = pl.ds(pl.multiple_of(g * BINS, BINS), BINS)
@@ -96,7 +100,7 @@
             out_ref[g] = jnp.zeros(out_ref.shape[1:], jnp.bfloat16)
 
 
-def whiten(traces, quality_local, forward):
+def whiten(traces, quality, forward):
     rows, seg, length = traces.shape
     pad = forward.shape[1]
     steps = 4
@@ -107,7 +111,7 @@
         in_specs=[
             pl.BlockSpec((2, pad // steps, length), lambda i: (0, i, 0)),
             pl.BlockSpec((seg, length, rows), lambda i: (0, 0, 0)),
-            pl.BlockSpec((1, cols), lambda i: (0, 0)),
+            pl.BlockSpec((quality.shape[1], rows), lambda i: (0, 0)),
         ],
         out_specs=pl.BlockSpec((pad // BINS, 2 * seg * BINS, rows), lambda i: (0, 0, 0)),
         out_shape=jax.ShapeDtypeStruct((pad // BINS, 2 * seg * BINS, rows), jnp.bfloat16),
@@ -117,7 +121,7 @@
         ],
         compiler_params=pltpu.CompilerParams(vmem_limit_bytes=VMEM),
         name="whiten",
-    )(forward, traces.transpose(1, 2, 0), quality_local)
+    )(forward, traces.transpose(1, 2, 0), quality.T)
 
 
 def other(a, bit):
@@ -126,7 +130,7 @@
 
 
 def stack_kernel(
-    blocks, white_ref, onehot_ref, inverse_ref, acc,
+    blocks, each, white_ref, index_ref, inverse_ref, acc,
     ybuf, xbuf, xf, cross, own_sem, y_send, y_recv, z_send, z_recv, p_send, p_recv,
 ):
     parts, _, depth, width = ybuf.shape
@@ -134,7 +138,6 @@
     _, chunks, rows16, lanes = xbuf.shape
     groups = GROUPS_STEP
     rep = groups * full // lanes
-    each = rows16 // rep
     nsrc = each * blocks
     outer = blocks // 2
     half_k = groups * BINS
@@ -208,7 +211,7 @@
         y_copy(c, 1).start()
         return carry
 
-    lax.fori_loop(0, chunks, start_own, 0)
+    lax.fori_loop(0, AHEAD, start_own, 0)
     own_copy().start()
     acc[...] = jnp.zeros_like(acc)
     own_copy().wait()
@@ -217,6 +220,13 @@
     lane = lax.broadcasted_iota(jnp.int32, (BINS, full), 1)
     row = lax.broadcasted_iota(jnp.int32, (BINS, full), 0)
     mask = lane % BINS == row
+
+    source = jnp.zeros((rows16, width), jnp.int32)
+    number = lax.broadcasted_iota(jnp.int32, (rows16, width), 0) % each
+    for n in range(each):
+        source = jnp.where(number == n, index_ref[n * blocks + b], source)
+    channel = b * width + lax.broadcasted_iota(jnp.int32, (rows16, width), 1)
+    onehot = jnp.where(source == channel, 1.0, 0.0).astype(jnp.bfloat16)
 
     def pick(c):
         for t in range(groups // rep):
@@ -224,7 +234,7 @@
             for sub in range(rep):
                 block = ybuf[:, c * groups + t * rep + sub].reshape(full, width)
                 part = lax.dot_general(
-                    onehot_ref[...], block, (((1,), (1,)), ((), ())),
+                    onehot, block, (((1,), (1,)), ((), ())),
                     preferred_element_type=jnp.float32,
                 )
                 found = part if sub == 0 else jnp.where(row16 // each == sub, part, found)
@@ -259,7 +269,7 @@
                 cross[:, pl.ds(half_k + at, 2 * BINS), :] = both[:, :, width:]
             return carry
 
-        lax.fori_loop(0, groups // rep, one_step, 0, unroll=2)
+        lax.fori_loop(0, groups // rep, one_step, 0, unroll=True)
 
     def invert(c):
         table = inverse_ref[c // INVERT]
@@ -274,6 +284,10 @@
         lax.fori_loop(0, nsrc // 2, add_pair, 0, unroll=4)
 
     def one_chunk(c, carry):
+        @pl.when(c < chunks - AHEAD)
+        def _():
+            start_own(c + AHEAD, 0)
+
         @pl.when(c < chunks)
         def _():
             y_wait(c, 0)
@@ -320,20 +334,21 @@
     lax.fori_loop(0, chunks, drain, 0)
 
 
-def stack(white, onehot, inverse, parts, blocks):
+def stack(white, src_index, inverse, parts, blocks):
     total, depth, rows = white.shape
     steps, taps, depth_k = inverse.shape
     chunks = steps * INVERT
-    nsrc = blocks * onehot.shape[0]
-    rep = 16 // onehot.shape[0]
+    nsrc = src_index.shape[0]
+    each = nsrc // blocks
+    rep = 16 // each
     lanes = GROUPS_STEP * parts * depth // rep
     outer = blocks // 2
     flops = 2 * nsrc * rows * total * (BINS * parts * depth * 2 + 2 * BINS * taps)
     return pl.pallas_call(
-        functools.partial(stack_kernel, blocks),
+        functools.partial(stack_kernel, blocks, each),
         in_specs=[
             pl.BlockSpec(memory_space=pl.ANY),
-            pl.BlockSpec(memory_space=pltpu.VMEM),
+            pl.BlockSpec(memory_space=pltpu.SMEM),
             pl.BlockSpec(memory_space=pltpu.VMEM),
         ],
         out_specs=pl.BlockSpec(memory_space=pltpu.VMEM),
@@ -356,14 +371,14 @@
         ),
         cost_estimate=pl.CostEstimate(flops=flops, bytes_accessed=20_000_000, transcendentals=0),
         name="stack",
-    )(white, jnp.tile(onehot, (rep, 1)), inverse)
+    )(white, src_index, inverse)
 
 
 def finish_kernel(acc_ref, out_ref):
     nlag = out_ref.shape[0]
-    for n in range(acc_ref.shape[0]):
-        count = acc_ref[n, nlag : nlag + 1, :]
-        out_ref[:, n, :] = acc_ref[n, :nlag, :] * (1.0 / jnp.maximum(count, 1.0))
+    value = acc_ref[...]
+    scale = 1.0 / jnp.maximum(value[:, nlag : nlag + 1, :], 1.0)
+    out_ref[...] = jnp.swapaxes(value * scale, 0, 1)[:nlag]
 
 
 def finish(acc):
@@ -380,19 +395,9 @@
 
 
 def on_device(parts, blocks, traces, src_index, quality):
-    rows, seg_local, length = traces.shape
-    nsrc = src_index.shape[0]
-    each = nsrc // blocks
-    forward, inverse = make_tables(length)
-    here, part = lax.axis_index("rcv"), lax.axis_index("src")
-    mine = lax.dynamic_slice_in_dim(quality.T, part * seg_local, seg_local, axis=0)
-    mine = mine.astype(jnp.float32).reshape(1, rows * seg_local)
-    white = whiten(traces, mine, jnp.asarray(forward))
-    own = lax.dynamic_index_in_dim(src_index.reshape(each, blocks), here, 1, keepdims=False)
-    onehot = (own[:, None] == here * rows + jnp.arange(rows, dtype=jnp.int32)[None, :]).astype(
-        jnp.bfloat16
-    )
-    return finish(stack(white, onehot, jnp.asarray(inverse), parts, blocks)).transpose(1, 0, 2)
+    forward, inverse = make_tables(traces.shape[2])
+    white = whiten(traces, quality, jnp.asarray(forward))
+    return finish(stack(white, src_index, jnp.asarray(inverse), parts, blocks)).transpose(1, 0, 2)
 
 
 def solution(mesh):

time: 106 us -> 108 us (1.019)
  Pallas kernels: 103 us -> 107 us
  local copies, waits for them, and re-layouts: 1.52 us -> 0 us
  other arithmetic: 1.36 us -> 0 us
    pallas_call x1, Pallas kernels: 83.2 us -> 88.3 us  [stack(): pl.pallas_call(functools.partial(stack_kernel, blocks, each), in_specs=[p...]
    convert_element_type x2 -> x0, other arithmetic: 1.36 us -> none  [the longest x1 1.28 us: on_device(): mine = mine.astype(jnp.float32).reshape(1, rows * seg_local)]
where the time goes in v4:
time: 108 us; the launch traced here: 107 us
  Pallas kernels  107 us (99%)
    pallas_call x1, Pallas kernels, stack(): pl.pallas_call(functools.partial(stack_kernel, blocks, each), in_specs=[p...  88.3 us
    pallas_call x1, Pallas kernels, whiten(): pl.pallas_call(functools.partial(whiten_kernel, length // 2, seg), grid=(...  10.5 us
    pallas_call x1, Pallas kernels, finish(): pl.pallas_call(finish_kernel, grid=(nsrc // tile,), in_specs=[pl.BlockSpe...  8.48 us

profile of v4, /device:TPU:0, one launch (start us, length us, event | category | flops | bytes accessed | tf_op | source)
XLA Modules:
  0.0 107.3 jit_solution(7924663558865978366)
XLA Ops:
  0.0 10.5 %whiten.1.white_ref = bf16[128,64,128]{2,1,0:T(8,128)(2,1)} custom-call(bf16[2,1024,2000]{2,1,0:T(8,128)(2,1)} %constant.4.clone.forward_ref, bf16[4,2000,128]{2,1,0:T(8,128)(2,1)} %bitcast.3, s32[16,128]{1,0:T(8,128)} %bitcast.4), custom_call_target="tpu_custom_call" | custom-call | tf_op jit(solution)/shard_map/whiten/pallas_call | solution.py:108
  10.5 88.3 %stack.1.acc_ref = f32[64,208,128]{2,1,0:T(8,128)} custom-call(bf16[128,64,128]{2,1,0:T(8,128)(2,1)} %whiten.1.white_ref, s32[64]{0:T(128)} %index_ref.1, bf16[4,208,512]{2,1,0:T(8,128)(2,1)} %constant.5.clone.inverse_ref), custom_call_target="tpu_custom_call" | custom-call | flops 15569256448 | bytes 20000000 | tf_op jit(solution)/shard_map/stack/pallas_call | solution.py:347
  98.8 8.5 %finish.1 = f32[201,64,128]{2,1,0:T(8,128)} custom-call(f32[64,208,128]{2,1,0:T(8,128)} %stack.1.acc_ref), custom_call_target="tpu_custom_call" | custom-call | tf_op jit(solution)/shard_map/finish/pallas_call | solution.py:387

commit v5 on v4

--- a/solution.py
+++ b/solution.py
@@ -12,9 +12,8 @@
 
 LAGH = 100
 BINS = 8
-GROUPS_STEP = 8
-INVERT = 4
-AHEAD = 4
+GROUPS_STEP = 16
+INVERT = 2
 VMEM = 60 * 1024 * 1024
 
 
@@ -211,7 +210,7 @@
         y_copy(c, 1).start()
         return carry
 
-    lax.fori_loop(0, AHEAD, start_own, 0)
+    lax.fori_loop(0, chunks, start_own, 0)
     own_copy().start()
     acc[...] = jnp.zeros_like(acc)
     own_copy().wait()
@@ -245,37 +244,32 @@
 
         def one_step(t, carry):
             cols = pl.ds(pl.multiple_of(t * full, full), full)
-            for s0 in range(0, rep, 2):
-                products = []
-                for sub in (s0, s0 + 1):
-                    y = ybuf[:, c * groups + t * rep + sub].reshape(parts, 2, depth // 2, width)
-                    turned = jnp.concatenate([-y[:, 1:], y[:, :1]], axis=1)
-                    right = jnp.concatenate(
-                        [y.reshape(full, width), turned.reshape(full, width)], axis=1
-                    )
-                    left = []
-                    for n in range(each):
-                        r = sub * each + n
-                        for k in range(blocks):
-                            left.append(jnp.where(mask, xf[k, r : r + 1, cols], 0.0))
-                    left = jnp.concatenate(left, axis=0)
-                    prod = jnp.dot(
-                        left.astype(jnp.bfloat16), right, preferred_element_type=jnp.float32
-                    )
-                    products.append(prod.reshape(nsrc, BINS, 2 * width))
-                both = jnp.concatenate(products, axis=1).astype(jnp.bfloat16)
-                at = pl.multiple_of(c % INVERT * 2 * half_k + (t * rep + s0) * BINS, 2 * BINS)
-                cross[:, pl.ds(at, 2 * BINS), :] = both[:, :, :width]
-                cross[:, pl.ds(half_k + at, 2 * BINS), :] = both[:, :, width:]
+            for sub in range(rep):
+                y = ybuf[:, c * groups + t * rep + sub].reshape(parts, 2, depth // 2, width)
+                turned = jnp.concatenate([-y[:, 1:], y[:, :1]], axis=1)
+                right = jnp.concatenate(
+                    [y.reshape(full, width), turned.reshape(full, width)], axis=1
+                )
+                left = []
+                for n in range(each):
+                    r = sub * each + n
+                    for k in range(blocks):
+                        left.append(jnp.where(mask, xf[k, r : r + 1, cols], 0.0))
+                left = jnp.concatenate(left, axis=0).astype(jnp.bfloat16)
+                prod = jnp.dot(left, right, preferred_element_type=jnp.float32)
+                prod = prod.reshape(nsrc, BINS, 2 * width)
+                at = pl.multiple_of(c % INVERT * 2 * half_k + (t * rep + sub) * BINS, BINS)
+                cross[:, pl.ds(at, BINS), :] = prod[:, :, :width]
+                cross[:, pl.ds(half_k + at, BINS), :] = prod[:, :, width:]
             return carry
 
-        lax.fori_loop(0, groups // rep, one_step, 0, unroll=True)
+        lax.fori_loop(0, groups // rep, one_step, 0, unroll=2)
 
     def invert(c):
         table = inverse_ref[c // INVERT]
 
         def add_pair(p, carry):
-            right = jnp.concatenate([cross[2 * p], cross[2 * p + 1]], axis=1)
+            right = jnp.concatenate([cross[2 * p], cross[2 * p + 1]], axis=1).astype(jnp.bfloat16)
             lagged = jnp.dot(table, right, preferred_element_type=jnp.float32)
             acc[2 * p] += lagged[:, :width]
             acc[2 * p + 1] += lagged[:, width:]
@@ -284,10 +278,6 @@
         lax.fori_loop(0, nsrc // 2, add_pair, 0, unroll=4)
 
     def one_chunk(c, carry):
-        @pl.when(c < chunks - AHEAD)
-        def _():
-            start_own(c + AHEAD, 0)
-
         @pl.when(c < chunks)
         def _():
             y_wait(c, 0)
@@ -357,7 +347,7 @@
             pltpu.VMEM((parts, total, depth, rows), jnp.bfloat16),
             pltpu.VMEM((blocks, chunks, 16, lanes), jnp.bfloat16),
             pltpu.VMEM((blocks, 16, lanes), jnp.float32),
-            pltpu.VMEM((nsrc, depth_k, rows), jnp.bfloat16),
+            pltpu.VMEM((nsrc, depth_k, rows), jnp.float32),
             pltpu.SemaphoreType.DMA,
             pltpu.SemaphoreType.DMA((chunks, 3)),
             pltpu.SemaphoreType.DMA((chunks, 3)),
@@ -383,13 +373,14 @@
 
 def finish(acc):
     nsrc, taps, rows = acc.shape
-    nlag, tile = 2 * LAGH + 1, 8
+    nlag, tile = 2 * LAGH + 1, 16
     return pl.pallas_call(
         finish_kernel,
         grid=(nsrc // tile,),
         in_specs=[pl.BlockSpec((tile, taps, rows), lambda i: (i, 0, 0))],
         out_specs=pl.BlockSpec((nlag, tile, rows), lambda i: (0, i, 0)),
         out_shape=jax.ShapeDtypeStruct((nlag, nsrc, rows), jnp.float32),
+        compiler_params=pltpu.CompilerParams(vmem_limit_bytes=VMEM),
         name="finish",
     )(acc)
 

time: 108 us -> 99.2 us (0.919)
  Pallas kernels: 107 us -> 98.9 us
    pallas_call x1, Pallas kernels: 88.3 us -> 81.8 us  [stack(): pl.pallas_call(functools.partial(stack_kernel, blocks, each), in_specs=[p...]
    pallas_call x1, Pallas kernels: 8.48 us -> 6.59 us  [finish(): pl.pallas_call(finish_kernel, grid=(nsrc // tile,), in_specs=[pl.BlockSpe...]
where the time goes in v5:
time: 99.2 us; the launch traced here: 98.9 us
  Pallas kernels  98.9 us (100%)
    pallas_call x1, Pallas kernels, stack(): pl.pallas_call(functools.partial(stack_kernel, blocks, each), in_specs=[p...  81.8 us
    pallas_call x1, Pallas kernels, whiten(): pl.pallas_call(functools.partial(whiten_kernel, length // 2, seg), grid=(...  10.5 us
    pallas_call x1, Pallas kernels, finish(): pl.pallas_call(finish_kernel, grid=(nsrc // tile,), in_specs=[pl.BlockSpe...  6.59 us

profile of v5, /device:TPU:0, one launch (start us, length us, event | category | flops | bytes accessed | tf_op | source)
XLA Modules:
  0.0 98.9 jit_solution(17805736265072403460)
XLA Ops:
  0.0 10.5 %whiten.1.white_ref = bf16[128,64,128]{2,1,0:T(8,128)(2,1)} custom-call(bf16[2,1024,2000]{2,1,0:T(8,128)(2,1)} %constant.4.clone.forward_ref, bf16[4,2000,128]{2,1,0:T(8,128)(2,1)} %bitcast.3, s32[16,128]{1,0:T(8,128)} %bitcast.4), custom_call_target="tpu_custom_call" | custom-call | tf_op jit(solution)/shard_map/whiten/pallas_call | solution.py:107
  10.5 81.8 %stack.1.acc_ref = f32[64,208,128]{2,1,0:T(8,128)} custom-call(bf16[128,64,128]{2,1,0:T(8,128)(2,1)} %whiten.1.white_ref, s32[64]{0:T(128)} %index_ref.1, bf16[4,208,512]{2,1,0:T(8,128)(2,1)} %constant.5.clone.inverse_ref), custom_call_target="tpu_custom_call" | custom-call | flops 15569256448 | bytes 20000000 | tf_op jit(solution)/shard_map/stack/pallas_call | solution.py:337
  92.3 6.6 %finish.1 = f32[201,64,128]{2,1,0:T(8,128)} custom-call(f32[64,208,128]{2,1,0:T(8,128)} %stack.1.acc_ref), custom_call_target="tpu_custom_call" | custom-call | tf_op jit(solution)/shard_map/finish/pallas_call | solution.py:377

commit v6 on v5

--- a/solution.py
+++ b/solution.py
@@ -12,8 +12,8 @@
 
 LAGH = 100
 BINS = 8
-GROUPS_STEP = 16
-INVERT = 2
+GROUPS_STEP = 8
+INVERT = 4
 VMEM = 60 * 1024 * 1024
 
 

time: 99.2 us -> 106 us (1.069)
  Pallas kernels: 98.9 us -> 106 us
    pallas_call x1, Pallas kernels: 81.8 us -> 89.1 us  [stack(): pl.pallas_call(functools.partial(stack_kernel, blocks, each), in_specs=[p...]
where the time goes in v6:
time: 106 us
  Pallas kernels  106 us (100%)
    pallas_call x1, Pallas kernels, stack(): pl.pallas_call(functools.partial(stack_kernel, blocks, each), in_specs=[p...  89.1 us
    pallas_call x1, Pallas kernels, whiten(): pl.pallas_call(functools.partial(whiten_kernel, length // 2, seg), grid=(...  10.5 us
    pallas_call x1, Pallas kernels, finish(): pl.pallas_call(finish_kernel, grid=(nsrc // tile,), in_specs=[pl.BlockSpe...  6.59 us

profile of v6, /device:TPU:0, one launch (start us, length us, event | category | flops | bytes accessed | tf_op | source)
XLA Modules:
  0.0 106.2 jit_solution(1444916724339145324)
XLA Ops:
  0.0 10.5 %whiten.1.white_ref = bf16[128,64,128]{2,1,0:T(8,128)(2,1)} custom-call(bf16[2,1024,2000]{2,1,0:T(8,128)(2,1)} %constant.4.clone.forward_ref, bf16[4,2000,128]{2,1,0:T(8,128)(2,1)} %bitcast.3, s32[16,128]{1,0:T(8,128)} %bitcast.4), custom_call_target="tpu_custom_call" | custom-call | tf_op jit(solution)/shard_map/whiten/pallas_call | solution.py:107
  10.5 89.1 %stack.1.acc_ref = f32[64,208,128]{2,1,0:T(8,128)} custom-call(bf16[128,64,128]{2,1,0:T(8,128)(2,1)} %whiten.1.white_ref, s32[64]{0:T(128)} %index_ref.1, bf16[4,208,512]{2,1,0:T(8,128)(2,1)} %constant.5.clone.inverse_ref), custom_call_target="tpu_custom_call" | custom-call | flops 15569256448 | bytes 20000000 | tf_op jit(solution)/shard_map/stack/pallas_call | solution.py:337
  99.6 6.6 %finish.1 = f32[201,64,128]{2,1,0:T(8,128)} custom-call(f32[64,208,128]{2,1,0:T(8,128)} %stack.1.acc_ref), custom_call_target="tpu_custom_call" | custom-call | tf_op jit(solution)/shard_map/finish/pallas_call | solution.py:377

commit v7 on v5

--- a/solution.py
+++ b/solution.py
@@ -130,11 +130,11 @@
 
 def stack_kernel(
     blocks, each, white_ref, index_ref, inverse_ref, acc,
-    ybuf, xbuf, xf, cross, own_sem, y_send, y_recv, z_send, z_recv, p_send, p_recv,
+    ybuf, xbuf, xf, cross, own_sem, core_sems, y_send, y_recv, z_send, z_recv, p_send, p_recv,
 ):
     parts, _, depth, width = ybuf.shape
     full = parts * depth
-    _, chunks, rows16, lanes = xbuf.shape
+    _, _, chunks, rows16, lanes = xbuf.shape
     groups = GROUPS_STEP
     rep = groups * full // lanes
     nsrc = each * blocks
@@ -167,7 +167,7 @@
 
     def y_copy(c, kind):
         at = groups_of(c)
-        if kind == 2:
+        if kind == 1:
             src, dst = ybuf.at[far, at], ybuf.at[far, at]
         else:
             src, dst = white_ref.at[at], ybuf.at[a, at]
@@ -177,39 +177,45 @@
 
     def y_wait(c, kind):
         at = groups_of(c)
-        got = (far, core, diag)[kind]
+        got = (far, diag)[kind]
         send(
             ybuf.at[got, at], ybuf.at[got, at], y_send.at[c, kind], y_recv.at[c, kind],
             {"src": far if kind == 0 else core},
         ).wait_recv()
 
+    def core_copy():
+        return send(white_ref, ybuf.at[a], core_sems.at[0], core_sems.at[1], {"src": core})
+
+    def core_wait():
+        send(
+            ybuf.at[core], ybuf.at[core], core_sems.at[0], core_sems.at[1], {"src": core}
+        ).wait_recv()
+
     def z_copy(c, d):
-        there = ((line + d) % outer) * 2 + side
-        return send(xbuf.at[b, c], xbuf.at[b, c], z_send.at[c, d], z_recv.at[c, d], {"rcv": there})
+        there = (line + d) % outer
+        block = xbuf.at[side, line, c]
+        return send(block, block, z_send.at[c, d], z_recv.at[c, d], {"rcv": there * 2 + side})
 
     def z_wait(c, d):
-        start = ((line + outer - d) % outer) * 2 + side
+        start = (line + outer - d) % outer
+        block = xbuf.at[side, start, c]
         send(
-            xbuf.at[start, c], xbuf.at[start, c], z_send.at[c, d], z_recv.at[c, d], {"rcv": start}
+            block, block, z_send.at[c, d], z_recv.at[c, d], {"rcv": start * 2 + side}
         ).wait_recv()
 
-    def p_copy(c, d):
-        start = ((line + outer - d) % outer) * 2 + side
-        return send(
-            xbuf.at[start, c], xbuf.at[start, c], p_send.at[c, d], p_recv.at[c, d], {"rcv": mate}
-        )
-
-    def p_wait(c, d):
-        start = ((line + outer - d) % outer) * 2 + 1 - side
-        send(
-            xbuf.at[start, c], xbuf.at[start, c], p_send.at[c, d], p_recv.at[c, d], {"rcv": mate}
-        ).wait_recv()
+    def p_copy(c):
+        block = xbuf.at[side, :, c]
+        return send(block, block, p_send.at[c], p_recv.at[c], {"rcv": mate})
+
+    def p_wait(c):
+        block = xbuf.at[1 - side, :, c]
+        send(block, block, p_send.at[c], p_recv.at[c], {"rcv": mate}).wait_recv()
 
     def start_own(c, carry):
         y_copy(c, 0).start()
-        y_copy(c, 1).start()
         return carry
 
+    core_copy().start()
     lax.fori_loop(0, chunks, start_own, 0)
     own_copy().start()
     acc[...] = jnp.zeros_like(acc)
@@ -237,10 +243,10 @@
                     preferred_element_type=jnp.float32,
                 )
                 found = part if sub == 0 else jnp.where(row16 // each == sub, part, found)
-            xbuf[b, c, :, t * full : (t + 1) * full] = found.astype(jnp.bfloat16)
+            xbuf[side, line, c, :, t * full : (t + 1) * full] = found.astype(jnp.bfloat16)
 
     def multiply(c):
-        xf[...] = xbuf[:, c].astype(jnp.float32)
+        xf[...] = xbuf[:, :, c].astype(jnp.float32)
 
         def one_step(t, carry):
             cols = pl.ds(pl.multiple_of(t * full, full), full)
@@ -254,7 +260,7 @@
                 for n in range(each):
                     r = sub * each + n
                     for k in range(blocks):
-                        left.append(jnp.where(mask, xf[k, r : r + 1, cols], 0.0))
+                        left.append(jnp.where(mask, xf[k % 2, k // 2, r : r + 1, cols], 0.0))
                 left = jnp.concatenate(left, axis=0).astype(jnp.bfloat16)
                 prod = jnp.dot(left, right, preferred_element_type=jnp.float32)
                 prod = prod.reshape(nsrc, BINS, 2 * width)
@@ -281,27 +287,25 @@
         @pl.when(c < chunks)
         def _():
             y_wait(c, 0)
-            y_copy(c, 2).start()
+            y_copy(c, 1).start()
 
         @pl.when(jnp.logical_and(c >= 1, c <= chunks))
         def _():
+            pl.when(c == 1)(core_wait)
             y_wait(c - 1, 1)
-            y_wait(c - 1, 2)
             pick(c - 1)
             for d in range(1, outer):
                 z_copy(c - 1, d).start()
-            p_copy(c - 1, 0).start()
 
         @pl.when(jnp.logical_and(c >= 2, c <= chunks + 1))
         def _():
             for d in range(1, outer):
                 z_wait(c - 2, d)
-                p_copy(c - 2, d).start()
+            p_copy(c - 2).start()
 
         @pl.when(c >= 3)
         def _():
-            for d in range(outer):
-                p_wait(c - 3, d)
+            p_wait(c - 3)
             multiply(c - 3)
 
             @pl.when((c - 3) % INVERT == INVERT - 1)
@@ -313,13 +317,14 @@
     lax.fori_loop(0, chunks + 3, one_chunk, 0)
 
     def drain(c, carry):
-        for kind in range(3):
+        for kind in range(2):
             y_copy(c, kind).wait_send()
         for d in range(1, outer):
             z_copy(c, d).wait_send()
-        for d in range(outer):
-            p_copy(c, d).wait_send()
+        p_copy(c).wait_send()
         return carry
+
+    core_copy().wait_send()
 
     lax.fori_loop(0, chunks, drain, 0)
 
@@ -345,16 +350,17 @@
         out_shape=jax.ShapeDtypeStruct((nsrc, taps, rows), jnp.float32),
         scratch_shapes=[
             pltpu.VMEM((parts, total, depth, rows), jnp.bfloat16),
-            pltpu.VMEM((blocks, chunks, 16, lanes), jnp.bfloat16),
-            pltpu.VMEM((blocks, 16, lanes), jnp.float32),
+            pltpu.VMEM((2, outer, chunks, 16, lanes), jnp.bfloat16),
+            pltpu.VMEM((2, outer, 16, lanes), jnp.float32),
             pltpu.VMEM((nsrc, depth_k, rows), jnp.float32),
             pltpu.SemaphoreType.DMA,
-            pltpu.SemaphoreType.DMA((chunks, 3)),
-            pltpu.SemaphoreType.DMA((chunks, 3)),
+            pltpu.SemaphoreType.DMA((2,)),
+            pltpu.SemaphoreType.DMA((chunks, 2)),
+            pltpu.SemaphoreType.DMA((chunks, 2)),
             pltpu.SemaphoreType.DMA((chunks, outer)),
             pltpu.SemaphoreType.DMA((chunks, outer)),
-            pltpu.SemaphoreType.DMA((chunks, outer)),
-            pltpu.SemaphoreType.DMA((chunks, outer)),
+            pltpu.SemaphoreType.DMA((chunks,)),
+            pltpu.SemaphoreType.DMA((chunks,)),
         ],
         compiler_params=pltpu.CompilerParams(
             vmem_limit_bytes=VMEM, collective_id=0, has_side_effects=True

time: 99.2 us -> 99.4 us (level)
  no operation moved by 1% of the time
where the time goes in v7:
time: 99.4 us; the launch traced here: 98.8 us
  Pallas kernels  98.8 us (99%)
    pallas_call x1, Pallas kernels, stack(): pl.pallas_call(functools.partial(stack_kernel, blocks, each), in_specs=[p...  81.7 us
    pallas_call x1, Pallas kernels, whiten(): pl.pallas_call(functools.partial(whiten_kernel, length // 2, seg), grid=(...  10.5 us
    pallas_call x1, Pallas kernels, finish(): pl.pallas_call(finish_kernel, grid=(nsrc // tile,), in_specs=[pl.BlockSpe...  6.59 us

profile of v7, /device:TPU:0, one launch (start us, length us, event | category | flops | bytes accessed | tf_op | source)
XLA Modules:
  0.0 98.8 jit_solution(3570034831147309098)
XLA Ops:
  0.0 10.5 %whiten.1.white_ref = bf16[128,64,128]{2,1,0:T(8,128)(2,1)} custom-call(bf16[2,1024,2000]{2,1,0:T(8,128)(2,1)} %constant.4.clone.forward_ref, bf16[4,2000,128]{2,1,0:T(8,128)(2,1)} %bitcast.3, s32[16,128]{1,0:T(8,128)} %bitcast.4), custom_call_target="tpu_custom_call" | custom-call | tf_op jit(solution)/shard_map/whiten/pallas_call | solution.py:107
  10.5 81.7 %stack.1.acc_ref = f32[64,208,128]{2,1,0:T(8,128)} custom-call(bf16[128,64,128]{2,1,0:T(8,128)(2,1)} %whiten.1.white_ref, s32[64]{0:T(128)} %index_ref.1, bf16[4,208,512]{2,1,0:T(8,128)(2,1)} %constant.5.clone.inverse_ref), custom_call_target="tpu_custom_call" | custom-call | flops 15569256448 | bytes 20000000 | tf_op jit(solution)/shard_map/stack/pallas_call | solution.py:342
  92.2 6.6 %finish.1 = f32[201,64,128]{2,1,0:T(8,128)} custom-call(f32[64,208,128]{2,1,0:T(8,128)} %stack.1.acc_ref), custom_call_target="tpu_custom_call" | custom-call | tf_op jit(solution)/shard_map/finish/pallas_call | solution.py:383

commit v8 on v5

--- a/solution.py
+++ b/solution.py
@@ -263,7 +263,7 @@
                 cross[:, pl.ds(half_k + at, BINS), :] = prod[:, :, width:]
             return carry
 
-        lax.fori_loop(0, groups // rep, one_step, 0, unroll=2)
+        lax.fori_loop(0, groups // rep, one_step, 0, unroll=4)
 
     def invert(c):
         table = inverse_ref[c // INVERT]
@@ -275,7 +275,7 @@
             acc[2 * p + 1] += lagged[:, width:]
             return carry
 
-        lax.fori_loop(0, nsrc // 2, add_pair, 0, unroll=4)
+        lax.fori_loop(0, nsrc // 2, add_pair, 0, unroll=8)
 
     def one_chunk(c, carry):
         @pl.when(c < chunks)

time: 99.2 us -> 96.8 us (0.976)
  Pallas kernels: 98.9 us -> 96.6 us
    pallas_call x1, Pallas kernels: 81.8 us -> 79.5 us  [stack(): pl.pallas_call(functools.partial(stack_kernel, blocks, each), in_specs=[p...]
where the time goes in v8:
time: 96.8 us; the launch traced here: 96.6 us
  Pallas kernels  96.6 us (100%)
    pallas_call x1, Pallas kernels, stack(): pl.pallas_call(functools.partial(stack_kernel, blocks, each), in_specs=[p...  79.5 us
    pallas_call x1, Pallas kernels, whiten(): pl.pallas_call(functools.partial(whiten_kernel, length // 2, seg), grid=(...  10.5 us
    pallas_call x1, Pallas kernels, finish(): pl.pallas_call(finish_kernel, grid=(nsrc // tile,), in_specs=[pl.BlockSpe...  6.59 us

profile of v8, /device:TPU:0, one launch (start us, length us, event | category | flops | bytes accessed | tf_op | source)
XLA Modules:
  0.0 96.6 jit_solution(15405847120300839485)
XLA Ops:
  0.0 10.5 %whiten.1.white_ref = bf16[128,64,128]{2,1,0:T(8,128)(2,1)} custom-call(bf16[2,1024,2000]{2,1,0:T(8,128)(2,1)} %constant.4.clone.forward_ref, bf16[4,2000,128]{2,1,0:T(8,128)(2,1)} %bitcast.3, s32[16,128]{1,0:T(8,128)} %bitcast.4), custom_call_target="tpu_custom_call" | custom-call | tf_op jit(solution)/shard_map/whiten/pallas_call | solution.py:107
  10.5 79.5 %stack.1.acc_ref = f32[64,208,128]{2,1,0:T(8,128)} custom-call(bf16[128,64,128]{2,1,0:T(8,128)(2,1)} %whiten.1.white_ref, s32[64]{0:T(128)} %index_ref.1, bf16[4,208,512]{2,1,0:T(8,128)(2,1)} %constant.5.clone.inverse_ref), custom_call_target="tpu_custom_call" | custom-call | flops 15569256448 | bytes 20000000 | tf_op jit(solution)/shard_map/stack/pallas_call | solution.py:337
  90.0 6.6 %finish.1 = f32[201,64,128]{2,1,0:T(8,128)} custom-call(f32[64,208,128]{2,1,0:T(8,128)} %stack.1.acc_ref), custom_call_target="tpu_custom_call" | custom-call | tf_op jit(solution)/shard_map/finish/pallas_call | solution.py:377
